TPU v7x, 512 devices: a whole 4x4x16 slice. The times are simulated.
512 devices in a mesh: tm: 8 (over x, y_hi), space: 64 (over z, y_lo, core).
Axes of the slice: x: 4, y: 4 (y_hi: 2, y_lo: 2; y = y_hi * 2 + y_lo), z: 16, core: 2. Of those that a mesh axis runs over, the one named last changes fastest.
Arguments:
- start_state: float32 [8, 2, 4096, 1024], P('tm', None, 'space'), may hold values from -6 to 6
- rigidity: float32 [4096, 1024], P('space'), may hold values from 0.5 to 2
- inv_mass: float32 [4096, 1024], P('space'), may hold values from 0.5 to 2
- gust_load: float32 [4096, 1024], P('space'), may hold values from -6 to 6
- kl_coeff: float32 [4, 4], replicated, may hold values from -3 to 3
- gust_history: float32 [32], P('tm'), may hold values from -4 to 4
Outputs:
- end_state: float32 [8, 2, 4096, 1024], P('tm', None, 'space')
All inputs are finite; a program needn't handle non-finite values.
Results may differ from a plain program's by a relative error of at most 0.000082.
Values sent between devices are 32-bit elements; how exact they have to be, the bound alone decides.
A program may use at most 64 MiB of HBM per device.

v0:
```python
import jax
import jax.numpy as jnp
from jax import lax
from jax.sharding import PartitionSpec as P

FINE = 4
ITERS = 2
KL = 4


STIFF_SCALE = 1.0 / 64.0
TIME_STEP = 0.18
HALF_STEP = 0.09
DAMPING = 0.05


def extended(block, sides, width):
    for axis, dim in sides:
        count = lax.axis_size(axis)
        forward = [(i, i + 1) for i in range(count - 1)]
        backward = [(target, source) for source, target in forward]
        low = lax.ppermute(
            lax.slice_in_dim(block, block.shape[dim] - width, None, axis=dim), axis, forward
        )
        high = lax.ppermute(lax.slice_in_dim(block, 0, width, axis=dim), axis, backward)
        block = jnp.concatenate([low, block, high], axis=dim)
    return block


def passed_along(block, axis, distance):
    devices = range(lax.axis_size(axis))
    route = [(i - distance, i) for i in devices if i - distance in devices]
    return lax.ppermute(block, axis, route)


def laplace(padded):
    return (
        padded[2:, 1:-1]
        + padded[:-2, 1:-1]
        + padded[1:-1, 2:]
        + padded[1:-1, :-2]
        - 4.0 * padded[1:-1, 1:-1]
    )


def mode_table(positions, extent):
    orders = (jnp.arange(KL) + 1).astype(jnp.float32)
    coords = (positions.astype(jnp.float32) + 0.5) / extent
    return jnp.cos(jnp.pi * orders[:, None] * coords[None, :])


def build_rigidity(rigidity, kl_coeff, first_row, extent_rows, extent_cols):
    row_count = rigidity.shape[0]
    col_count = rigidity.shape[1]
    across = mode_table(first_row + jnp.arange(row_count), extent_rows)
    along_chord = mode_table(jnp.arange(col_count), extent_cols)
    mixed = jnp.dot(kl_coeff, along_chord, precision=lax.Precision.HIGHEST)
    kl_field = jnp.dot(across.T, mixed, precision=lax.Precision.HIGHEST)
    return rigidity * jnp.exp(0.5 * jnp.tanh(kl_field))


def apply_padded(widened, rigid_rim):
    weighted = rigid_rim * laplace(jnp.pad(widened, ((0, 0), (1, 1))))
    return STIFF_SCALE * laplace(jnp.pad(weighted, ((0, 0), (1, 1))))


def accelerate(velocity, stiff_now, inv_mass, gust_load, gust_value):
    return inv_mass * (gust_load * gust_value - stiff_now) - DAMPING * velocity


def coarse_step(position, velocity, stiff_now, inv_mass, gust_load, gust_value):
    coarse_span = FINE * TIME_STEP
    new_vel = velocity + coarse_span * accelerate(
        velocity, stiff_now, inv_mass, gust_load, gust_value
    )
    return (position + coarse_span * new_vel, new_vel)


def per_device(start_state, rigidity, inv_mass, gust_load, kl_coeff, gust_history):
    row_count = rigidity.shape[0]
    col_count = rigidity.shape[1]
    space_count = lax.axis_size("space")
    time_count = lax.axis_size("tm")
    time_slot = lax.axis_index("tm")
    space_slot = lax.axis_index("space")
    stiff_field = build_rigidity(
        rigidity, kl_coeff, space_slot * row_count, row_count * space_count, col_count
    )
    rigid_one = extended(stiff_field, (("space", 0),), 1)

    def fine_stiff(moved):
        widened = extended(moved, (("space", 0),), 2)
        return apply_padded(widened, rigid_one)

    def coarse_stiff(moved):
        widened = extended(moved, (("space", 0),), 2)
        return apply_padded(widened, rigid_one)

    def coarse_move(position, velocity, stiff_now, gust_value):
        return coarse_step(position, velocity, stiff_now, inv_mass, gust_load, gust_value)

    position = start_state[0, 0]
    velocity = start_state[0, 1]
    end_pos = position
    end_vel = velocity
    for sweep_index in range(ITERS):
        last_sweep = sweep_index == ITERS - 1
        fine_position = position
        fine_velocity = velocity
        fine_stiff_now = fine_stiff(fine_position)
        first_stiff = fine_stiff_now
        for step_index in range(FINE):
            fine_gust_value = gust_history[step_index]
            half_vel = fine_velocity + HALF_STEP * accelerate(
                fine_velocity, fine_stiff_now, inv_mass, gust_load, fine_gust_value
            )
            fine_position = fine_position + TIME_STEP * half_vel
            fine_stiff_now = fine_stiff(fine_position)
            fine_velocity = half_vel + HALF_STEP * accelerate(
                half_vel, fine_stiff_now, inv_mass, gust_load, fine_gust_value
            )
        fine_pos, fine_vel, first_stiff = (fine_position, fine_velocity, first_stiff)
        coarse_pos, coarse_vel = coarse_move(position, velocity, first_stiff, gust_history[0])
        delta_pos = fine_pos - coarse_pos
        delta_vel = fine_vel - coarse_vel
        chain_pos = position
        chain_vel = velocity
        for turn_index in range(1, time_count):
            stiff_now = coarse_stiff(chain_pos)
            moved_pos, moved_vel = coarse_move(chain_pos, chain_vel, stiff_now, gust_history[0])
            outgoing = jnp.stack([moved_pos + delta_pos, moved_vel + delta_vel])
            arrived = passed_along(outgoing, "tm", 1)
            chain_pos = jnp.where(time_slot == turn_index, arrived[0], chain_pos)
            chain_vel = jnp.where(time_slot == turn_index, arrived[1], chain_vel)
        if last_sweep:
            stiff_now = coarse_stiff(chain_pos)
            moved_pos, moved_vel = coarse_move(chain_pos, chain_vel, stiff_now, gust_history[0])
            end_pos = moved_pos + delta_pos
            end_vel = moved_vel + delta_vel
        position = chain_pos
        velocity = chain_vel
    return jnp.stack([end_pos, end_vel])[None]


def solution(mesh):
    in_specs = (
        P("tm", None, "space", None),
        P("space", None),
        P("space", None),
        P("space", None),
        P(),
        P("tm"),
    )
    out_specs = P("tm", None, "space", None)
    return jax.shard_map(
        per_device, mesh=mesh, in_specs=in_specs, out_specs=out_specs, check_vma=False
    )
```

profile of v0, /device:TPU:7, one launch (start us, length us, event | category | flops | bytes accessed | tf_op | source)
XLA Modules:
  0.0 458.3 jit_solution(7215187144377704200)
XLA Ops:
  56.2 11.7 %collective-permute-done.12 = f32[2,64,1024]{2,1,0:T(8,128)S(1)} collective-permute-done((f32[2,64,1024]{2,1,0:T(8,128)S(1)}, f32[2,64,1024]{2,1,0:T(8,128)S(1)}, u32[]{:S(2)}, u32[]{:S(2)}) %collective-permute-start.12) | collective-permute-done | bytes 524320 | tf_op jit(solution)/shard_map/ppermute | solution.py:33
  81.3 11.6 %collective-permute-done.15 = f32[2,64,1024]{2,1,0:T(8,128)S(1)} collective-permute-done((f32[2,64,1024]{2,1,0:T(8,128)S(1)}, f32[2,64,1024]{2,1,0:T(8,128)S(1)}, u32[]{:S(2)}, u32[]{:S(2)}) %collective-permute-start.15) | collective-permute-done | bytes 524320 | tf_op jit(solution)/shard_map/ppermute | solution.py:33
  94.8 5.7 %collective-permute-start.17 = (f32[2,1024]{1,0:T(2,128)S(1)}, f32[2,1024]{1,0:T(2,128)S(1)}, u32[]{:S(2)}, u32[]{:S(2)}) collective-permute-start(f32[2,1024]{1,0:T(2,128)S(1)} %get-tuple-element.98), channel_id=1, source_target_pairs={{0,1},{1,2},{2,3},{3,4},{4,5},{5,6},{6,7},{7,8},{8,9},{9,10},{10,1... | collective-permute-start | bytes 24584 | tf_op jit(solution)/shard_map/ppermute | solution.py:22
  106.4 12.4 %collective-permute-done.18 = f32[2,64,1024]{2,1,0:T(8,128)S(1)} collective-permute-done((f32[2,64,1024]{2,1,0:T(8,128)}, f32[2,64,1024]{2,1,0:T(8,128)S(1)}, u32[]{:S(2)}, u32[]{:S(2)}) %collective-permute-start.18) | collective-permute-done | bytes 524320 | tf_op jit(solution)/shard_map/ppermute | solution.py:33
  129.4 14.4 %collective-permute-done.21 = f32[2,64,1024]{2,1,0:T(8,128)S(1)} collective-permute-done((f32[2,64,1024]{2,1,0:T(8,128)S(1)}, f32[2,64,1024]{2,1,0:T(8,128)S(1)}, u32[]{:S(2)}, u32[]{:S(2)}) %collective-permute-start.21) | collective-permute-done | bytes 524320 | tf_op jit(solution)/shard_map/ppermute | solution.py:33
  154.2 15.5 %collective-permute-done.24 = f32[2,64,1024]{2,1,0:T(8,128)S(1)} collective-permute-done((f32[2,64,1024]{2,1,0:T(8,128)}, f32[2,64,1024]{2,1,0:T(8,128)S(1)}, u32[]{:S(2)}, u32[]{:S(2)}) %collective-permute-start.24) | collective-permute-done | bytes 524320 | tf_op jit(solution)/shard_map/ppermute | solution.py:33
  179.3 15.4 %collective-permute-done.27 = f32[2,64,1024]{2,1,0:T(8,128)S(1)} collective-permute-done((f32[2,64,1024]{2,1,0:T(8,128)S(1)}, f32[2,64,1024]{2,1,0:T(8,128)S(1)}, u32[]{:S(2)}, u32[]{:S(2)}) %collective-permute-start.27) | collective-permute-done | bytes 524320 | tf_op jit(solution)/shard_map/ppermute | solution.py:33
  204.3 15.4 %collective-permute-done.30 = f32[2,64,1024]{2,1,0:T(8,128)S(1)} collective-permute-done((f32[2,64,1024]{2,1,0:T(8,128)S(1)}, f32[2,64,1024]{2,1,0:T(8,128)S(1)}, u32[]{:S(2)}, u32[]{:S(2)}) %collective-permute-start.30) | collective-permute-done | bytes 524320 | tf_op jit(solution)/shard_map/ppermute | solution.py:33
  229.8 8.5 %collective-permute-start.34 = (f32[2,1024]{1,0:T(2,128)S(1)}, f32[2,1024]{1,0:T(2,128)S(1)}, u32[]{:S(2)}, u32[]{:S(2)}) collective-permute-start(f32[2,1024]{1,0:T(2,128)S(1)} %get-tuple-element.86), channel_id=1, source_target_pairs={{0,1},{1,2},{2,3},{3,4},{4,5},{5,6},{6,7},{7,8},{8,9},{9,10},{10,1... | collective-permute-start | bytes 24584 | tf_op jit(solution)/shard_map/ppermute | solution.py:22
  242.8 9.2 %collective-permute-start.36 = (f32[2,1024]{1,0:T(2,128)S(1)}, f32[2,1024]{1,0:T(2,128)S(1)}, u32[]{:S(2)}, u32[]{:S(2)}) collective-permute-start(f32[2,1024]{1,0:T(2,128)S(1)} %get-tuple-element.84), channel_id=1, source_target_pairs={{0,1},{1,2},{2,3},{3,4},{4,5},{5,6},{6,7},{7,8},{8,9},{9,10},{10,1... | collective-permute-start | bytes 24584 | tf_op jit(solution)/shard_map/ppermute | solution.py:22
  275.4 13.8 %collective-permute-done.41 = f32[2,64,1024]{2,1,0:T(8,128)S(1)} collective-permute-done((f32[2,64,1024]{2,1,0:T(8,128)S(1)}, f32[2,64,1024]{2,1,0:T(8,128)S(1)}, u32[]{:S(2)}, u32[]{:S(2)}) %collective-permute-start.41) | collective-permute-done | bytes 524320 | tf_op jit(solution)/shard_map/ppermute | solution.py:33
  291.2 6.2 %collective-permute-start.43 = (f32[2,1024]{1,0:T(2,128)S(1)}, f32[2,1024]{1,0:T(2,128)S(1)}, u32[]{:S(2)}, u32[]{:S(2)}) collective-permute-start(f32[2,1024]{1,0:T(2,128)S(1)} %get-tuple-element.78), channel_id=1, source_target_pairs={{0,1},{1,2},{2,3},{3,4},{4,5},{5,6},{6,7},{7,8},{8,9},{9,10},{10,1... | collective-permute-start | bytes 24584 | tf_op jit(solution)/shard_map/ppermute | solution.py:22
  301.3 12.8 %collective-permute-done.44 = f32[2,64,1024]{2,1,0:T(8,128)S(1)} collective-permute-done((f32[2,64,1024]{2,1,0:T(8,128)S(1)}, f32[2,64,1024]{2,1,0:T(8,128)S(1)}, u32[]{:S(2)}, u32[]{:S(2)}) %collective-permute-start.44) | collective-permute-done | bytes 524320 | tf_op jit(solution)/shard_map/ppermute | solution.py:33
  316.1 6.5 %collective-permute-start.46 = (f32[2,1024]{1,0:T(2,128)S(1)}, f32[2,1024]{1,0:T(2,128)S(1)}, u32[]{:S(2)}, u32[]{:S(2)}) collective-permute-start(f32[2,1024]{1,0:T(2,128)S(1)} %get-tuple-element.76), channel_id=1, source_target_pairs={{0,1},{1,2},{2,3},{3,4},{4,5},{5,6},{6,7},{7,8},{8,9},{9,10},{10,1... | collective-permute-start | bytes 24584 | tf_op jit(solution)/shard_map/ppermute | solution.py:22
  326.6 12.4 %collective-permute-done.47 = f32[2,64,1024]{2,1,0:T(8,128)S(1)} collective-permute-done((f32[2,64,1024]{2,1,0:T(8,128)S(1)}, f32[2,64,1024]{2,1,0:T(8,128)S(1)}, u32[]{:S(2)}, u32[]{:S(2)}) %collective-permute-start.47) | collective-permute-done | bytes 524320 | tf_op jit(solution)/shard_map/ppermute | solution.py:33
  341.0 6.9 %collective-permute-start.49 = (f32[2,1024]{1,0:T(2,128)S(1)}, f32[2,1024]{1,0:T(2,128)S(1)}, u32[]{:S(2)}, u32[]{:S(2)}) collective-permute-start(f32[2,1024]{1,0:T(2,128)S(1)} %get-tuple-element.74), channel_id=1, source_target_pairs={{0,1},{1,2},{2,3},{3,4},{4,5},{5,6},{6,7},{7,8},{8,9},{9,10},{10,1... | collective-permute-start | bytes 24584 | tf_op jit(solution)/shard_map/ppermute | solution.py:22
  351.9 12.0 %collective-permute-done.50 = f32[2,64,1024]{2,1,0:T(8,128)S(1)} collective-permute-done((f32[2,64,1024]{2,1,0:T(8,128)S(1)}, f32[2,64,1024]{2,1,0:T(8,128)S(1)}, u32[]{:S(2)}, u32[]{:S(2)}) %collective-permute-start.50) | collective-permute-done | bytes 524320 | tf_op jit(solution)/shard_map/ppermute | solution.py:33
  365.9 7.9 %collective-permute-start.52 = (f32[2,1024]{1,0:T(2,128)S(1)}, f32[2,1024]{1,0:T(2,128)S(1)}, u32[]{:S(2)}, u32[]{:S(2)}) collective-permute-start(f32[2,1024]{1,0:T(2,128)S(1)} %get-tuple-element.72), channel_id=1, source_target_pairs={{0,1},{1,2},{2,3},{3,4},{4,5},{5,6},{6,7},{7,8},{8,9},{9,10},{10,1... | collective-permute-start | bytes 24584 | tf_op jit(solution)/shard_map/ppermute | solution.py:22
  377.8 11.0 %collective-permute-done.53 = f32[2,64,1024]{2,1,0:T(8,128)S(1)} collective-permute-done((f32[2,64,1024]{2,1,0:T(8,128)S(1)}, f32[2,64,1024]{2,1,0:T(8,128)S(1)}, u32[]{:S(2)}, u32[]{:S(2)}) %collective-permute-start.53) | collective-permute-done | bytes 524320 | tf_op jit(solution)/shard_map/ppermute | solution.py:33
  390.8 9.9 %collective-permute-start.55 = (f32[2,1024]{1,0:T(2,128)S(1)}, f32[2,1024]{1,0:T(2,128)S(1)}, u32[]{:S(2)}, u32[]{:S(2)}) collective-permute-start(f32[2,1024]{1,0:T(2,128)S(1)} %get-tuple-element.70), channel_id=1, source_target_pairs={{0,1},{1,2},{2,3},{3,4},{4,5},{5,6},{6,7},{7,8},{8,9},{9,10},{10,1... | collective-permute-start | bytes 24584 | tf_op jit(solution)/shard_map/ppermute | solution.py:22
  404.7 10.4 %collective-permute-done.56 = f32[2,64,1024]{2,1,0:T(8,128)S(1)} collective-permute-done((f32[2,64,1024]{2,1,0:T(8,128)S(1)}, f32[2,64,1024]{2,1,0:T(8,128)S(1)}, u32[]{:S(2)}, u32[]{:S(2)}) %collective-permute-start.56) | collective-permute-done | bytes 524320 | tf_op jit(solution)/shard_map/ppermute | solution.py:33
  417.1 11.1 %collective-permute-start.58 = (f32[2,1024]{1,0:T(2,128)S(1)}, f32[2,1024]{1,0:T(2,128)S(1)}, u32[]{:S(2)}, u32[]{:S(2)}) collective-permute-start(f32[2,1024]{1,0:T(2,128)S(1)} %get-tuple-element.68), channel_id=1, source_target_pairs={{0,1},{1,2},{2,3},{3,4},{4,5},{5,6},{6,7},{7,8},{8,9},{9,10},{10,1... | collective-permute-start | bytes 24584 | tf_op jit(solution)/shard_map/ppermute | solution.py:22
  432.2 10.4 %collective-permute-done.59 = f32[2,64,1024]{2,1,0:T(8,128)S(1)} collective-permute-done((f32[2,64,1024]{2,1,0:T(8,128)S(1)}, f32[2,64,1024]{2,1,0:T(8,128)S(1)}, u32[]{:S(2)}, u32[]{:S(2)}) %collective-permute-start.59) | collective-permute-done | bytes 524320 | tf_op jit(solution)/shard_map/ppermute | solution.py:33
  444.6 10.9 %collective-permute-start.61 = (f32[2,1024]{1,0:T(2,128)S(1)}, f32[2,1024]{1,0:T(2,128)S(1)}, u32[]{:S(2)}, u32[]{:S(2)}) collective-permute-start(f32[2,1024]{1,0:T(2,128)S(1)} %get-tuple-element.66), channel_id=1, source_target_pairs={{0,1},{1,2},{2,3},{3,4},{4,5},{5,6},{6,7},{7,8},{8,9},{9,10},{10,1... | collective-permute-start | bytes 24584 | tf_op jit(solution)/shard_map/ppermute | solution.py:22
  (254 shorter events, 194.8 us)
Async XLA Ops:
  2.8 12.7 %collective-permute-start = (f32[1,1024]{1,0:T(1,128)S(1)}, f32[1,1024]{1,0:T(1,128)S(1)}, u32[]{:S(2)}, u32[]{:S(2)}) collective-permute-start(f32[1,1024]{1,0:T(1,128)S(1)} %get-tuple-element.110), channel_id=1, source_target_pairs={{0,1},{1,2},{2,3},{3,4},{4,5},{5,6},{6,7},{7,8},{8,9},{9,10},{10,1... | collective-permute-start | bytes 12296 | tf_op jit(solution)/shard_map/ppermute | solution.py:22
  51.4 16.6 %collective-permute-start.12 = (f32[2,64,1024]{2,1,0:T(8,128)S(1)}, f32[2,64,1024]{2,1,0:T(8,128)S(1)}, u32[]{:S(2)}, u32[]{:S(2)}) collective-permute-start(f32[2,64,1024]{2,1,0:T(8,128)S(1)} %pad_maximum_fusion), channel_id=1, source_target_pairs={{0,64},{64,128},{128,192},{192,256},{256,320},{320,384},{384,448},... | collective-permute-start | bytes 1572872 | tf_op jit(solution)/shard_map/ppermute | solution.py:33
  77.4 15.5 %collective-permute-start.15 = (f32[2,64,1024]{2,1,0:T(8,128)S(1)}, f32[2,64,1024]{2,1,0:T(8,128)S(1)}, u32[]{:S(2)}, u32[]{:S(2)}) collective-permute-start(f32[2,64,1024]{2,1,0:T(8,128)S(1)} %pad_maximum_fusion.1), channel_id=1, source_target_pairs={{0,64},{64,128},{128,192},{192,256},{256,320},{320,384},{384,448},... | collective-permute-start | bytes 1572872 | tf_op jit(solution)/shard_map/ppermute | solution.py:33
  103.4 15.4 %collective-permute-start.18 = (f32[2,64,1024]{2,1,0:T(8,128)}, f32[2,64,1024]{2,1,0:T(8,128)S(1)}, u32[]{:S(2)}, u32[]{:S(2)}) collective-permute-start(f32[2,64,1024]{2,1,0:T(8,128)} %pad_maximum_fusion.2), channel_id=1, source_target_pairs={{0,64},{64,128},{128,192},{192,256},{256,320},{320,384},{384,448},... | collective-permute-start | bytes 1572872 | tf_op jit(solution)/shard_map/ppermute | solution.py:33
  127.2 16.6 %collective-permute-start.21 = (f32[2,64,1024]{2,1,0:T(8,128)S(1)}, f32[2,64,1024]{2,1,0:T(8,128)S(1)}, u32[]{:S(2)}, u32[]{:S(2)}) collective-permute-start(f32[2,64,1024]{2,1,0:T(8,128)S(1)} %pad_maximum_fusion.3), channel_id=1, source_target_pairs={{0,64},{64,128},{128,192},{192,256},{256,320},{320,384},{384,448},... | collective-permute-start | bytes 1572872 | tf_op jit(solution)/shard_map/ppermute | solution.py:33
  152.2 17.4 %collective-permute-start.24 = (f32[2,64,1024]{2,1,0:T(8,128)}, f32[2,64,1024]{2,1,0:T(8,128)S(1)}, u32[]{:S(2)}, u32[]{:S(2)}) collective-permute-start(f32[2,64,1024]{2,1,0:T(8,128)} %pad_maximum_fusion.4), channel_id=1, source_target_pairs={{0,64},{64,128},{128,192},{192,256},{256,320},{320,384},{384,448},... | collective-permute-start | bytes 1572872 | tf_op jit(solution)/shard_map/ppermute | solution.py:33
  177.4 17.3 %collective-permute-start.27 = (f32[2,64,1024]{2,1,0:T(8,128)S(1)}, f32[2,64,1024]{2,1,0:T(8,128)S(1)}, u32[]{:S(2)}, u32[]{:S(2)}) collective-permute-start(f32[2,64,1024]{2,1,0:T(8,128)S(1)} %pad_maximum_fusion.5), channel_id=1, source_target_pairs={{0,64},{64,128},{128,192},{192,256},{256,320},{320,384},{384,448},... | collective-permute-start | bytes 1572872 | tf_op jit(solution)/shard_map/ppermute | solution.py:33
  202.4 17.3 %collective-permute-start.30 = (f32[2,64,1024]{2,1,0:T(8,128)S(1)}, f32[2,64,1024]{2,1,0:T(8,128)S(1)}, u32[]{:S(2)}, u32[]{:S(2)}) collective-permute-start(f32[2,64,1024]{2,1,0:T(8,128)S(1)} %pad_maximum_fusion.6), channel_id=1, source_target_pairs={{0,64},{64,128},{128,192},{192,256},{256,320},{320,384},{384,448},... | collective-permute-start | bytes 1572872 | tf_op jit(solution)/shard_map/ppermute | solution.py:33
  227.9 10.4 %collective-permute-start.33 = (f32[2,1024]{1,0:T(2,128)S(1)}, f32[2,1024]{1,0:T(2,128)S(1)}, u32[]{:S(2)}, u32[]{:S(2)}) collective-permute-start(f32[2,1024]{1,0:T(2,128)S(1)} %get-tuple-element.87), channel_id=1, source_target_pairs={{1,0},{2,1},{3,2},{4,3},{5,4},{6,5},{7,6},{8,7},{9,8},{10,9},{11,1... | collective-permute-start | bytes 24584 | tf_op jit(solution)/shard_map/ppermute | solution.py:25
  240.9 11.2 %collective-permute-start.35 = (f32[2,1024]{1,0:T(2,128)S(1)}, f32[2,1024]{1,0:T(2,128)S(1)}, u32[]{:S(2)}, u32[]{:S(2)}) collective-permute-start(f32[2,1024]{1,0:T(2,128)S(1)} %get-tuple-element.85), channel_id=1, source_target_pairs={{1,0},{2,1},{3,2},{4,3},{5,4},{6,5},{7,6},{8,7},{9,8},{10,9},{11,1... | collective-permute-start | bytes 24584 | tf_op jit(solution)/shard_map/ppermute | solution.py:25
  242.8 10.0 %collective-permute-start.36 = (f32[2,1024]{1,0:T(2,128)S(1)}, f32[2,1024]{1,0:T(2,128)S(1)}, u32[]{:S(2)}, u32[]{:S(2)}) collective-permute-start(f32[2,1024]{1,0:T(2,128)S(1)} %get-tuple-element.84), channel_id=1, source_target_pairs={{0,1},{1,2},{2,3},{3,4},{4,5},{5,6},{6,7},{7,8},{8,9},{9,10},{10,1... | collective-permute-start | bytes 24584 | tf_op jit(solution)/shard_map/ppermute | solution.py:22
  273.4 15.8 %collective-permute-start.41 = (f32[2,64,1024]{2,1,0:T(8,128)S(1)}, f32[2,64,1024]{2,1,0:T(8,128)S(1)}, u32[]{:S(2)}, u32[]{:S(2)}) collective-permute-start(f32[2,64,1024]{2,1,0:T(8,128)S(1)} %pad_maximum_fusion.7), channel_id=1, source_target_pairs={{0,64},{64,128},{128,192},{192,256},{256,320},{320,384},{384,448},... | collective-permute-start | bytes 1572872 | tf_op jit(solution)/shard_map/ppermute | solution.py:33
  299.4 14.7 %collective-permute-start.44 = (f32[2,64,1024]{2,1,0:T(8,128)S(1)}, f32[2,64,1024]{2,1,0:T(8,128)S(1)}, u32[]{:S(2)}, u32[]{:S(2)}) collective-permute-start(f32[2,64,1024]{2,1,0:T(8,128)S(1)} %pad_maximum_fusion.8), channel_id=1, source_target_pairs={{0,64},{64,128},{128,192},{192,256},{256,320},{320,384},{384,448},... | collective-permute-start | bytes 1572872 | tf_op jit(solution)/shard_map/ppermute | solution.py:33
  324.6 14.4 %collective-permute-start.47 = (f32[2,64,1024]{2,1,0:T(8,128)S(1)}, f32[2,64,1024]{2,1,0:T(8,128)S(1)}, u32[]{:S(2)}, u32[]{:S(2)}) collective-permute-start(f32[2,64,1024]{2,1,0:T(8,128)S(1)} %pad_maximum_fusion.9), channel_id=1, source_target_pairs={{0,64},{64,128},{128,192},{192,256},{256,320},{320,384},{384,448},... | collective-permute-start | bytes 1572872 | tf_op jit(solution)/shard_map/ppermute | solution.py:33
  350.0 13.9 %collective-permute-start.50 = (f32[2,64,1024]{2,1,0:T(8,128)S(1)}, f32[2,64,1024]{2,1,0:T(8,128)S(1)}, u32[]{:S(2)}, u32[]{:S(2)}) collective-permute-start(f32[2,64,1024]{2,1,0:T(8,128)S(1)} %pad_maximum_fusion.10), channel_id=1, source_target_pairs={{0,64},{64,128},{128,192},{192,256},{256,320},{320,384},{384,448},... | collective-permute-start | bytes 1572872 | tf_op jit(solution)/shard_map/ppermute | solution.py:33
  375.9 12.9 %collective-permute-start.53 = (f32[2,64,1024]{2,1,0:T(8,128)S(1)}, f32[2,64,1024]{2,1,0:T(8,128)S(1)}, u32[]{:S(2)}, u32[]{:S(2)}) collective-permute-start(f32[2,64,1024]{2,1,0:T(8,128)S(1)} %pad_maximum_fusion.11), channel_id=1, source_target_pairs={{0,64},{64,128},{128,192},{192,256},{256,320},{320,384},{384,448},... | collective-permute-start | bytes 1572872 | tf_op jit(solution)/shard_map/ppermute | solution.py:33
  388.9 11.9 %collective-permute-start.54 = (f32[2,1024]{1,0:T(2,128)S(1)}, f32[2,1024]{1,0:T(2,128)S(1)}, u32[]{:S(2)}, u32[]{:S(2)}) collective-permute-start(f32[2,1024]{1,0:T(2,128)S(1)} %get-tuple-element.71), channel_id=1, source_target_pairs={{1,0},{2,1},{3,2},{4,3},{5,4},{6,5},{7,6},{8,7},{9,8},{10,9},{11,1... | collective-permute-start | bytes 24584 | tf_op jit(solution)/shard_map/ppermute | solution.py:25
  390.8 10.7 %collective-permute-start.55 = (f32[2,1024]{1,0:T(2,128)S(1)}, f32[2,1024]{1,0:T(2,128)S(1)}, u32[]{:S(2)}, u32[]{:S(2)}) collective-permute-start(f32[2,1024]{1,0:T(2,128)S(1)} %get-tuple-element.70), channel_id=1, source_target_pairs={{0,1},{1,2},{2,3},{3,4},{4,5},{5,6},{6,7},{7,8},{8,9},{9,10},{10,1... | collective-permute-start | bytes 24584 | tf_op jit(solution)/shard_map/ppermute | solution.py:22
  402.8 12.3 %collective-permute-start.56 = (f32[2,64,1024]{2,1,0:T(8,128)S(1)}, f32[2,64,1024]{2,1,0:T(8,128)S(1)}, u32[]{:S(2)}, u32[]{:S(2)}) collective-permute-start(f32[2,64,1024]{2,1,0:T(8,128)S(1)} %pad_maximum_fusion.12), channel_id=1, source_target_pairs={{0,64},{64,128},{128,192},{192,256},{256,320},{320,384},{384,448},... | collective-permute-start | bytes 1572872 | tf_op jit(solution)/shard_map/ppermute | solution.py:33
  415.2 13.0 %collective-permute-start.57 = (f32[2,1024]{1,0:T(2,128)S(1)}, f32[2,1024]{1,0:T(2,128)S(1)}, u32[]{:S(2)}, u32[]{:S(2)}) collective-permute-start(f32[2,1024]{1,0:T(2,128)S(1)} %get-tuple-element.69), channel_id=1, source_target_pairs={{1,0},{2,1},{3,2},{4,3},{5,4},{6,5},{7,6},{8,7},{9,8},{10,9},{11,1... | collective-permute-start | bytes 24584 | tf_op jit(solution)/shard_map/ppermute | solution.py:25
  417.1 11.8 %collective-permute-start.58 = (f32[2,1024]{1,0:T(2,128)S(1)}, f32[2,1024]{1,0:T(2,128)S(1)}, u32[]{:S(2)}, u32[]{:S(2)}) collective-permute-start(f32[2,1024]{1,0:T(2,128)S(1)} %get-tuple-element.68), channel_id=1, source_target_pairs={{0,1},{1,2},{2,3},{3,4},{4,5},{5,6},{6,7},{7,8},{8,9},{9,10},{10,1... | collective-permute-start | bytes 24584 | tf_op jit(solution)/shard_map/ppermute | solution.py:22
  430.3 12.3 %collective-permute-start.59 = (f32[2,64,1024]{2,1,0:T(8,128)S(1)}, f32[2,64,1024]{2,1,0:T(8,128)S(1)}, u32[]{:S(2)}, u32[]{:S(2)}) collective-permute-start(f32[2,64,1024]{2,1,0:T(8,128)S(1)} %pad_maximum_fusion.13), channel_id=1, source_target_pairs={{0,64},{64,128},{128,192},{192,256},{256,320},{320,384},{384,448},... | collective-permute-start | bytes 1572872 | tf_op jit(solution)/shard_map/ppermute | solution.py:33
  442.6 12.8 %collective-permute-start.60 = (f32[2,1024]{1,0:T(2,128)S(1)}, f32[2,1024]{1,0:T(2,128)S(1)}, u32[]{:S(2)}, u32[]{:S(2)}) collective-permute-start(f32[2,1024]{1,0:T(2,128)S(1)} %get-tuple-element.67), channel_id=1, source_target_pairs={{1,0},{2,1},{3,2},{4,3},{5,4},{6,5},{7,6},{8,7},{9,8},{10,9},{11,1... | collective-permute-start | bytes 24584 | tf_op jit(solution)/shard_map/ppermute | solution.py:25
  444.6 11.7 %collective-permute-start.61 = (f32[2,1024]{1,0:T(2,128)S(1)}, f32[2,1024]{1,0:T(2,128)S(1)}, u32[]{:S(2)}, u32[]{:S(2)}) collective-permute-start(f32[2,1024]{1,0:T(2,128)S(1)} %get-tuple-element.66), channel_id=1, source_target_pairs={{0,1},{1,2},{2,3},{3,4},{4,5},{5,6},{6,7},{7,8},{8,9},{9,10},{10,1... | collective-permute-start | bytes 24584 | tf_op jit(solution)/shard_map/ppermute | solution.py:22
  (44 other events, 256.7 us)
where the time goes:
time: 465 us; the launch traced here: 458 us
  starting transfers between devices  221 us (48%)
  waiting for transfers between devices  196 us (42%)
  other arithmetic  35.1 us (8%)
    ppermute x14, waiting for transfers between devices, passed_along(): return lax.ppermute(block, axis, route)  179 us
    ppermute x24, starting transfers between devices, extended(): lax.ppermute(lax.slice_in_dim(block, block.shape[dim] - width, None, axis...  142 us
    ppermute x24, starting transfers between devices, extended(): lax.ppermute(lax.slice_in_dim(block, 0, width, axis=dim), axis, backward)  46.1 us
    ppermute x14, starting transfers between devices, passed_along(): return lax.ppermute(block, axis, route)  33.1 us
    another operation x42, other arithmetic, per_device(): outgoing = jnp.stack([moved_pos + delta_pos, moved_vel + delta_vel])  19 us
    ppermute x24, waiting for transfers between devices, extended(): lax.ppermute(lax.slice_in_dim(block, block.shape[dim] - width, None, axis...  16.6 us
  transfers between devices with their start and end apart: 62, of which 36 were waited for; matrix products, arithmetic and copies ran while one was open for 0% of the time, Pallas kernels for 0%

commit v1 on v0

v1 whole, which is shorter than its diff:
```python
import functools

import jax
import jax.numpy as jnp
import numpy as np
from jax import lax
from jax.experimental import pallas as pl
from jax.experimental.pallas import tpu as pltpu
from jax.sharding import PartitionSpec as P

FINE = 4
KL = 4
STIFF_SCALE = 1.0 / 64.0
TIME_STEP = 0.18
HALF_STEP = 0.09
DAMPING = 0.05
COARSE = FINE * TIME_STEP
KEEP = 1.0 - HALF_STEP * DAMPING
KEEP_COARSE = 1.0 - COARSE * DAMPING
RATIO = COARSE / HALF_STEP

HALO = 32
STRIP = 128
ROWS = 64
REGION = STRIP + 2 * HALO
PAD = 8
HALF = REGION // 2
MESH = pl.DeviceIdType.MESH


def kernel(
    tcount,
    scount,
    state,
    rigidity,
    inv_mass,
    gust_load,
    kl_coeff,
    gust,
    cos_x,
    cos_y,
    out,
    state_v,
    coef_v,
    cosx_v,
    cosy_v,
    turned,
    halo_up,
    halo_down,
    coef_t,
    got_core,
    got_up,
    got_down,
    got_gust,
    coef_up,
    coef_down,
    gust_row,
    stiff,
    kick,
    load,
    pos,
    vel,
    weighted,
    diff_p,
    diff_q,
    first_k,
    corr,
    outgoing,
    incoming,
    result,
    local_sem,
    send_sem,
    recv_sem,
    coef_send,
    coef_recv,
    back_send,
    back_recv,
):
    t = lax.axis_index("tm")
    s = lax.axis_index("space")
    has_low = s > 0
    has_high = s < scount - 1
    last = tcount - 1

    load_state = pltpu.make_async_copy(state, state_v, local_sem.at[0])
    load_state.start()
    loads = [
        pltpu.make_async_copy(src, dst, local_sem.at[1 + i])
        for i, (src, dst) in enumerate(
            [
                (rigidity, coef_v.at[0]),
                (inv_mass, coef_v.at[1]),
                (gust_load, coef_v.at[2]),
                (cos_x.at[s], cosx_v),
                (cos_y.at[t], cosy_v),
            ]
        )
    ]
    for copy in loads:
        copy.start()

    barrier = pltpu.get_barrier_semaphore()

    def greet(tt, ss):
        pl.semaphore_signal(barrier, inc=1, device_id=(tt, ss), device_id_type=MESH)

    for i in range(1, tcount):
        greet(lax.rem(t + i, tcount), s)

    @pl.when(has_low)
    def _():
        for i in range(tcount):
            greet(lax.rem(t + i, tcount), s - 1)

    @pl.when(has_high)
    def _():
        for i in range(tcount):
            greet(lax.rem(t + i, tcount), s + 1)

    lane = lax.broadcasted_iota(jnp.int32, (8, 128), 1)

    def lanes(rows):
        return lax.broadcasted_iota(jnp.int32, (rows, 128), 1)

    zero_halo = jnp.zeros((HALO, 128), jnp.float32)
    turned[0:HALO, :] = zero_halo
    turned[HALO + tcount * STRIP :, :] = zero_halo
    load_state.wait()
    for i in range(tcount):
        turned[HALO + i * STRIP : HALO + (i + 1) * STRIP, :] = state_v[
            :, i * STRIP : (i + 1) * STRIP
        ].T

    row8 = lax.broadcasted_iota(jnp.int32, (8, 128), 0)
    gust_block = jnp.zeros((8, 128), jnp.float32)
    for i in range(FINE):
        gust_block = jnp.where(row8 == i, gust[i], gust_block)
    gust_row[...] = gust_block

    packed = halo_up.shape[0]
    first_quarter = lax.rem(lanes(packed), 64) < 32
    near = turned[0:packed, :]
    far = turned[HALF : HALF + packed, :]
    halo_up[...] = jnp.where(first_quarter, near, pltpu.roll(far, 32, 1))
    halo_down[...] = jnp.where(first_quarter, pltpu.roll(far, 96, 1), near)

    pl.semaphore_wait(
        barrier,
        tcount - 1 + tcount * has_low.astype(jnp.int32) + tcount * has_high.astype(jnp.int32),
    )

    def remote(src, dst, send, recv, tt, ss):
        return pltpu.make_async_remote_copy(
            src_ref=src,
            dst_ref=dst,
            send_sem=send,
            recv_sem=recv,
            device_id=(tt, ss),
            device_id_type=MESH,
        )

    def strip_of(tt, rows):
        return pl.ds(pl.multiple_of(tt * STRIP, STRIP), rows)

    def core_copy(tt, slot):
        return remote(
            turned.at[strip_of(tt, REGION)], got_core.at[slot], send_sem.at[0, tt], recv_sem.at[0, slot], tt, s
        )

    def up_copy(tt, slot):
        return remote(
            halo_up.at[strip_of(tt, HALF)], got_up.at[slot], send_sem.at[1, tt], recv_sem.at[1, slot], tt, s - 1
        )

    def down_copy(tt, slot):
        return remote(
            halo_down.at[strip_of(tt, HALF)], got_down.at[slot], send_sem.at[2, tt], recv_sem.at[2, slot], tt, s + 1
        )

    def gust_copy(tt, slot):
        return remote(gust_row, got_gust.at[slot], send_sem.at[3, tt], recv_sem.at[3, slot], tt, s)

    @pl.when(t < last)
    def _():
        for i in range(1, tcount + 1):
            tt = lax.rem(t + i, tcount)
            if i < tcount:
                core_copy(tt, t).start()

            @pl.when(has_low)
            def _():
                up_copy(tt, t).start()

            @pl.when(has_high)
            def _():
                down_copy(tt, t).start()

    for i in range(1, tcount):
        gust_copy(lax.rem(t + i, tcount), t).start()

    for copy in loads:
        copy.wait()

    def turn_coef(tile, first, rows, target):
        cols = pl.ds(pl.multiple_of(tile * STRIP, STRIP), STRIP)
        pair = jnp.concatenate([coef_v[0, :, cols], coef_v[1, :, cols]], axis=0).T
        other = jnp.concatenate([coef_v[2, :, cols], coef_v[2, :, cols]], axis=0).T
        coef_t[0, target : target + rows, :] = pair[first : first + rows]
        coef_t[1, target : target + rows, :] = other[first : first + rows]

    turn_coef(t, 0, STRIP, HALO)

    @pl.when(t > 0)
    def _():
        turn_coef(t - 1, STRIP - HALO, HALO, 0)

    @pl.when(t == 0)
    def _():
        coef_t[0, 0:HALO, :] = zero_halo
        coef_t[1, 0:HALO, :] = zero_halo

    @pl.when(t < last)
    def _():
        turn_coef(t + 1, 0, HALO, HALO + STRIP)

    @pl.when(t == last)
    def _():
        coef_t[0, HALO + STRIP :, :] = zero_halo
        coef_t[1, HALO + STRIP :, :] = zero_halo

    coef_low = remote(coef_t, coef_up, coef_send.at[0], coef_recv.at[0], t, s - 1)
    coef_high = remote(coef_t, coef_down, coef_send.at[1], coef_recv.at[1], t, s + 1)

    @pl.when(has_low)
    def _():
        coef_low.start()

    @pl.when(has_high)
    def _():
        coef_high.start()

    @pl.when(jnp.logical_not(has_low))
    def _():
        coef_down[...] = jnp.zeros_like(coef_down)
        got_down[...] = jnp.zeros_like(got_down)

    @pl.when(jnp.logical_not(has_high))
    def _():
        coef_up[...] = jnp.zeros_like(coef_up)
        got_up[...] = jnp.zeros_like(got_up)

    mixed = []
    for b in range(KL):
        row = kl_coeff[0, b] * cosx_v[0:1, :]
        for a in range(1, KL):
            row = row + kl_coeff[a, b] * cosx_v[a : a + 1, :]
        mixed.append(row)
    mixed = jnp.concatenate(mixed + [jnp.zeros((128 - KL, 128), jnp.float32)], axis=0)
    field = jnp.dot(
        cosy_v[...], mixed, precision=lax.Precision.HIGHEST, preferred_element_type=jnp.float32
    )
    factor = STIFF_SCALE * jnp.exp(0.5 * jnp.tanh(field))

    zero_pad = jnp.zeros((PAD, 128), jnp.float32)
    for buf in (pos, weighted, corr):
        for i in range(buf.shape[0]):
            buf[i, 0:PAD, :] = zero_pad
            buf[i, PAD + REGION :, :] = zero_pad
    for i in range(diff_p.shape[0]):
        diff_p[i, 0:PAD, :] = zero_pad
        diff_p[i, PAD + REGION :, :] = zero_pad

    @pl.when(has_high)
    def _():
        remote(coef_t, coef_up, coef_send.at[0], coef_recv.at[0], t, s + 1).wait_recv()

    @pl.when(has_low)
    def _():
        remote(coef_t, coef_down, coef_send.at[1], coef_recv.at[1], t, s - 1).wait_recv()

    all_lanes = lanes(REGION)
    core_lanes = all_lanes < ROWS
    up_lanes = all_lanes < ROWS + HALO

    def assemble(core, up, down):
        return jnp.where(core_lanes, core, jnp.where(up_lanes, up, down))

    own_pair, own_load = coef_t[0], coef_t[1]
    up_pair, up_load = coef_up[0], coef_up[1]
    down_pair, down_load = coef_down[0], coef_down[1]
    rig = assemble(own_pair, pltpu.roll(up_pair, 64, 1), pltpu.roll(down_pair, 64, 1))
    mass = assemble(pltpu.roll(own_pair, 64, 1), up_pair, down_pair)
    gload = assemble(own_load, up_load, down_load)
    stiff[...] = rig * factor
    kick[...] = HALF_STEP * mass
    load[...] = (HALF_STEP * mass) * gload

    def laplace(ref, slot, lo, hi):
        centre = ref[slot, PAD + lo : PAD + hi, :]
        rows = ref[slot, PAD + lo - 1 : PAD + hi - 1, :] + ref[slot, PAD + lo + 1 : PAD + hi + 1, :]
        sides = pltpu.roll(centre, 1, 1) + pltpu.roll(centre, 127, 1)
        return (rows + sides) - 4.0 * centre

    def stiffness(ref, slot, scratch, lo, hi):
        wlo, whi = max(lo - 8, 0), min(hi + 8, REGION)
        weighted[scratch, PAD + wlo : PAD + whi, :] = stiff[wlo:whi, :] * laplace(ref, slot, wlo, whi)
        return laplace(weighted, scratch, lo, hi)

    def fine(slot, scratch, spring, velocity, g, lows):
        lo = lows[0]
        hi = REGION - lo
        half = KEEP * velocity - kick[lo:hi, :] * spring + load[lo:hi, :] * g[0]
        pos[slot, PAD + lo : PAD + hi, :] += TIME_STEP * half
        vel[slot, lo:hi, :] = half
        for i in range(1, FINE):
            lo = lows[i]
            hi = REGION - lo
            spring = stiffness(pos, slot, scratch, lo, hi)
            half = (
                (KEEP * KEEP) * vel[slot, lo:hi, :]
                - (1.0 + KEEP) * (kick[lo:hi, :] * spring)
                + load[lo:hi, :] * (KEEP * g[i - 1] + g[i])
            )
            pos[slot, PAD + lo : PAD + hi, :] += TIME_STEP * half
            vel[slot, lo:hi, :] = half
        lo = lows[FINE]
        hi = REGION - lo
        spring = stiffness(pos, slot, scratch, lo, hi)
        return (
            pos[slot, PAD + lo : PAD + hi, :],
            KEEP * vel[slot, lo:hi, :] - kick[lo:hi, :] * spring + load[lo:hi, :] * g[FINE - 1],
        )

    def gusts(n):
        return [got_gust[n, i : i + 1, :] for i in range(FINE)]

    def own_copies():
        return (
            pltpu.make_async_copy(turned.at[strip_of(t, REGION)], got_core.at[t], local_sem.at[6]),
            pltpu.make_async_copy(gust_row, got_gust.at[t], local_sem.at[7]),
        )

    for copy in own_copies():
        copy.start()

    def first_sweep(i, carry):
        n = lax.rem(t - i + tcount, tcount)

        @pl.when(i > 0)
        def _():
            gust_copy(n, n).wait_recv()

        @pl.when(i == 0)
        def _():
            own_copies()[1].wait()
            own_copies()[0].wait()

        @pl.when(jnp.logical_and(i > 0, n < last))
        def _():
            core_copy(n, n).wait_recv()

        @pl.when(jnp.logical_and(has_high, n < last))
        def _():
            up_copy(n, n).wait_recv()

        @pl.when(jnp.logical_and(has_low, n < last))
        def _():
            down_copy(n, n).wait_recv()

        @pl.when(n < last)
        def _():
            sub = lanes(HALF)
            core_sub = sub < ROWS
            up_sub = sub < ROWS + HALO
            for part in range(2):
                first = part * HALF
                core = got_core[n, first : first + HALF, :]
                up = got_up[n]
                down = got_down[n]
                turn = [(64, 64, 0, 0), (32, 96, 96, 32)][part]
                p_up, p_down, q_up, q_down = [
                    v if k == 0 else pltpu.roll(v, k, 1)
                    for v, k in zip((up, down, up, down), turn)
                ]
                pos[0, PAD + first : PAD + first + HALF, :] = jnp.where(
                    core_sub, core, jnp.where(up_sub, p_up, p_down)
                )
                vel[0, first : first + HALF, :] = jnp.where(
                    core_sub, pltpu.roll(core, 64, 1), jnp.where(up_sub, q_up, q_down)
                )
            share = jnp.where(n > 0, 1.0, 0.0)
            spring = stiffness(pos, 0, 0, 0, REGION)
            coarse_q = KEEP_COARSE * vel[0] - RATIO * (kick[...] * spring)
            diff_q[n] = -share * coarse_q
            diff_p[n, PAD : PAD + REGION, :] = -share * (pos[0, PAD : PAD + REGION, :] + COARSE * coarse_q)
            new_p, new_q = fine(0, 0, spring, vel[0], gusts(n), (0, 0, 0, 8, 8))
            diff_p[n, PAD + 8 : PAD + REGION - 8, :] += new_p
            diff_q[n, 8 : REGION - 8, :] += new_q

        return carry

    lax.fori_loop(0, tcount, first_sweep, 0)

    def down8(value):
        return value // 8 * 8

    for n in range(1, tcount - 1):
        lo = down8(10 + 2 * n)
        hi = REGION - lo
        spring = stiffness(diff_p, n - 1, n % 2, lo, hi)
        first_k[n, lo:hi, :] = spring
        coarse_q = KEEP_COARSE * diff_q[n - 1, lo:hi, :] - RATIO * (kick[lo:hi, :] * spring)
        diff_q[n, lo:hi, :] += coarse_q
        diff_p[n, PAD + lo : PAD + hi, :] += diff_p[n - 1, PAD + lo : PAD + hi, :] + COARSE * coarse_q

    own = slice(HALO, HALO + STRIP)
    own_padded = slice(PAD + HALO, PAD + HALO + STRIP)
    own_lanes = lanes(STRIP) < ROWS

    def back_copy(n, slot):
        return remote(outgoing.at[n], incoming.at[slot], back_send.at[n], back_recv.at[slot], n, s)

    def send_back(n, p_own, q_own):
        outgoing[n] = jnp.where(own_lanes, p_own, pltpu.roll(q_own, 64, 1))

        @pl.when(t != n)
        def _():
            back_copy(n, t).start()

    send_back(0, diff_p[0, own_padded, :], diff_q[0, own, :])

    for n in range(1, tcount):
        slot = n % 2
        before = n - 1
        lows = [down8(10 + 2 * n + 2 * k) for k in range(FINE + 1)]
        lo = lows[0]
        hi = REGION - lo
        pos[slot, PAD + lo - 8 : PAD + hi + 8, :] = diff_p[before, PAD + lo - 8 : PAD + hi + 8, :]
        if n < tcount - 1:
            spring = first_k[n, lo:hi, :]
        else:
            spring = stiffness(pos, slot, slot, lo, hi)
        new_p, new_q = fine(slot, slot, spring, diff_q[before, lo:hi, :], gusts(n), lows)
        lo = lows[FINE]
        hi = REGION - lo
        if n > 1:
            spring = stiffness(corr, slot, 2, lo, hi)
            coarse_q = KEEP_COARSE * first_k[0, lo:hi, :] - RATIO * (kick[lo:hi, :] * spring)
            new_q = new_q + coarse_q
            new_p = new_p + (corr[slot, PAD + lo : PAD + hi, :] + COARSE * coarse_q)
        if n < tcount - 1:
            corr[1 - slot, PAD + lo : PAD + hi, :] = new_p - diff_p[n, PAD + lo : PAD + hi, :]
            first_k[0, lo:hi, :] = new_q - diff_q[n, lo:hi, :]
        off = HALO - lo
        send_back(n, new_p[off : off + STRIP], new_q[off : off + STRIP])

    def place(tt, block):
        cols = pl.ds(pl.multiple_of(tt * STRIP, STRIP), STRIP)
        result[:, cols] = block.T

    place(t, outgoing[t])
    for i in range(1, tcount):
        tt = lax.rem(t + i, tcount)
        back_copy(tt, tt).wait_recv()
        place(tt, incoming[tt])
    store = pltpu.make_async_copy(result, out, local_sem.at[0])
    store.start()

    for i in range(1, tcount):
        tt = lax.rem(t + i, tcount)
        back_copy(tt, t).wait_send()
        gust_copy(tt, t).wait_send()

    @pl.when(t < last)
    def _():
        for i in range(1, tcount + 1):
            tt = lax.rem(t + i, tcount)
            if i < tcount:
                core_copy(tt, t).wait_send()

            @pl.when(has_low)
            def _():
                up_copy(tt, t).wait_send()

            @pl.when(has_high)
            def _():
                down_copy(tt, t).wait_send()

    @pl.when(has_low)
    def _():
        coef_low.wait_send()

    @pl.when(has_high)
    def _():
        coef_high.wait_send()

    store.wait()


def tables(tcount, scount, rows, cols):
    orders = np.arange(1, KL + 1)
    lane = np.arange(128)
    along = np.where(lane < ROWS + HALO, lane, lane - 128)
    x = np.arange(scount)[:, None] * ROWS + along[None, :]
    y = np.arange(tcount)[:, None] * STRIP - HALO + np.arange(REGION)[None, :]
    cos_x = np.zeros((scount, 8, 128), np.float32)
    cos_x[:, :KL] = np.cos(np.pi * orders[None, :, None] * ((x[:, None, :] + 0.5) / rows))
    cos_y = np.zeros((tcount, REGION, 128), np.float32)
    cos_y[:, :, :KL] = np.cos(np.pi * orders[None, None, :] * ((y[:, :, None] + 0.5) / cols))
    return cos_x, cos_y


def per_device(tcount, scount, start_state, rigidity, inv_mass, gust_load, kl_coeff, gust_history):
    rows, cols = rigidity.shape
    cos_x, cos_y = tables(tcount, scount, rows * scount, cols)
    f32 = jnp.float32
    padded = PAD + REGION + PAD
    packed = (tcount - 1) * STRIP + HALF
    vmem = pltpu.VMEM
    dma = pltpu.SemaphoreType.DMA
    anywhere = pl.BlockSpec(memory_space=pl.ANY)
    scalars = pl.BlockSpec(memory_space=pltpu.SMEM)
    result = pl.pallas_call(
        functools.partial(kernel, tcount, scount),
        out_shape=jax.ShapeDtypeStruct((2 * rows, cols), f32),
        in_specs=[anywhere] * 4 + [scalars] * 2 + [anywhere] * 2,
        out_specs=anywhere,
        scratch_shapes=[
            vmem((2 * rows, cols), f32),
            vmem((3, rows, cols), f32),
            vmem((8, 128), f32),
            vmem((REGION, 128), f32),
            vmem((2 * HALO + tcount * STRIP, 128), f32),
            vmem((packed, 128), f32),
            vmem((packed, 128), f32),
            vmem((2, REGION, 128), f32),
            vmem((tcount, REGION, 128), f32),
            vmem((tcount, HALF, 128), f32),
            vmem((tcount, HALF, 128), f32),
            vmem((tcount, 8, 128), f32),
            vmem((2, REGION, 128), f32),
            vmem((2, REGION, 128), f32),
            vmem((8, 128), f32),
            vmem((REGION, 128), f32),
            vmem((REGION, 128), f32),
            vmem((REGION, 128), f32),
            vmem((2, padded, 128), f32),
            vmem((2, REGION, 128), f32),
            vmem((3, padded, 128), f32),
            vmem((tcount - 1, padded, 128), f32),
            vmem((tcount - 1, REGION, 128), f32),
            vmem((tcount - 1, REGION, 128), f32),
            vmem((2, padded, 128), f32),
            vmem((tcount, STRIP, 128), f32),
            vmem((tcount, STRIP, 128), f32),
            vmem((2 * rows, cols), f32),
            dma((8,)),
            dma((4, tcount)),
            dma((4, tcount)),
            dma((2,)),
            dma((2,)),
            dma((tcount,)),
            dma((tcount,)),
        ],
        compiler_params=pltpu.CompilerParams(
            collective_id=0, has_side_effects=True, vmem_limit_bytes=32 * 1024 * 1024
        ),
    )(
        start_state.reshape(2 * rows, cols),
        rigidity,
        inv_mass,
        gust_load,
        kl_coeff,
        gust_history,
        jnp.asarray(cos_x),
        jnp.asarray(cos_y),
    )
    return result.reshape(1, 2, rows, cols)


def solution(mesh):
    in_specs = (
        P("tm", None, "space", None),
        P("space", None),
        P("space", None),
        P("space", None),
        P(),
        P("tm"),
    )
    return jax.shard_map(
        functools.partial(per_device, mesh.shape["tm"], mesh.shape["space"]),
        mesh=mesh,
        in_specs=in_specs,
        out_specs=P("tm", None, "space", None),
        check_vma=False,
    )
```

time: 465 us -> 62.1 us (0.13); the launches traced: 458 us -> 61.8 us
  starting transfers between devices: 221 us -> 0 us
  waiting for transfers between devices: 196 us -> 0 us
  Pallas kernels: 0 us -> 53.6 us
  other arithmetic: 35.1 us -> 0 us
  local copies, waits for them, and re-layouts: 2.92 us -> 8.1 us
    ppermute x62 -> x0, starting transfers between devices: 221 us -> none  [the longest x24 142 us: extended(): lax.ppermute(lax.slice_in_dim(block, block.shape[dim] - width, None, axis...]
    ppermute x62 -> x0, waiting for transfers between devices: 196 us -> none  [the longest x14 179 us: passed_along(): return lax.ppermute(block, axis, route)]
    pallas_call x0 -> x1, Pallas kernels: none -> 53.6 us  [per_device(): pl.pallas_call(functools.partial(kernel, tcount, scount), out_shape=jax.S...]
    another operation x44 -> x0, other arithmetic: 20 us -> none  [the longest x42 19 us: per_device(): outgoing = jnp.stack([moved_pos + delta_pos, moved_vel + delta_vel])]
    add x6 -> x0, other arithmetic: 7.79 us -> none  [per_device(): fine_position = fine_position + TIME_STEP * half_vel]
    unnamed x12 -> x17, local copies, waits for them, and re-layouts: 2.04 us -> 8.1 us
    mul x24 -> x0, other arithmetic: 5.34 us -> none  [the longest x23 5.33 us: apply_padded(): weighted = rigid_rim * laplace(jnp.pad(widened, ((0, 0), (1, 1))))]
  transfers between devices with their start and end apart: 62 -> 0, of which waited for: 36 -> 0; matrix products, arithmetic and copies ran while one was open for 0% -> 0% of each run, Pallas kernels for 0% -> 0%
where the time goes in v1:
time: 62.1 us; the launch traced here: 61.8 us
  Pallas kernels  53.6 us (86%)
  local copies, waits for them, and re-layouts  8.1 us (13%)
    pallas_call x1, Pallas kernels, per_device(): pl.pallas_call(functools.partial(kernel, tcount, scount), out_shape=jax.S...  53.6 us
    unnamed x17, local copies, waits for them, and re-layouts  8.1 us

profile of v1, /device:TPU:7, one launch (start us, length us, event | category | flops | bytes accessed | tf_op | source)
XLA Modules:
  0.0 61.8 jit_solution(8089137572759468605)
XLA Ops:
  0.0 0.0 copy-start.7
  0.0 0.7 %copy-done.7 = f32[4]{0:T(128)S(1)} copy-done((f32[4]{0:T(128)S(1)}, f32[4]{0:T(128)}, u32[]{:S(2)}) %copy-start.7) | copy-done | bytes 40
  0.7 0.0 copy-start
  0.7 1.1 %copy-done = f32[8,192,128]{2,1,0:T(8,128)S(1)} copy-done((f32[8,192,128]{2,1,0:T(8,128)S(1)}, f32[8,192,128]{2,1,0:T(8,128)}, u32[]{:S(2)}) %copy-start) | copy-done | bytes 786456
  1.8 0.0 copy-start.1
  1.8 1.0 %copy-done.1 = f32[1,2,64,1024]{3,2,1,0:T(8,128)S(1)} copy-done((f32[1,2,64,1024]{3,2,1,0:T(8,128)S(1)}, f32[1,2,64,1024]{3,2,1,0:T(8,128)}, u32[]{:S(2)}) %copy-start.1) | copy-done | bytes 524312
  2.8 0.0 copy-start.2
  2.8 0.9 %copy-done.2 = f32[64,1024]{1,0:T(8,128)S(1)} copy-done((f32[64,1024]{1,0:T(8,128)S(1)}, f32[64,1024]{1,0:T(8,128)}, u32[]{:S(2)}) %copy-start.2) | copy-done | bytes 262168
  3.8 0.0 copy-start.3
  3.8 0.9 %copy-done.3 = f32[64,1024]{1,0:T(8,128)S(1)} copy-done((f32[64,1024]{1,0:T(8,128)S(1)}, f32[64,1024]{1,0:T(8,128)}, u32[]{:S(2)}) %copy-start.3) | copy-done | bytes 262168
  4.7 0.0 copy-start.4
  4.7 0.9 %copy-done.4 = f32[64,1024]{1,0:T(8,128)S(1)} copy-done((f32[64,1024]{1,0:T(8,128)S(1)}, f32[64,1024]{1,0:T(8,128)}, u32[]{:S(2)}) %copy-start.4) | copy-done | bytes 262168
  5.7 0.0 copy-start.5
  5.7 0.9 %copy-done.5 = f32[64,8,128]{2,1,0:T(8,128)S(1)} copy-done((f32[64,8,128]{2,1,0:T(8,128)S(1)}, f32[64,8,128]{2,1,0:T(8,128)}, u32[]{:S(2)}) %copy-start.5) | copy-done | bytes 262168
  6.6 0.0 copy-start.6
  6.6 0.7 %copy-done.6 = f32[4,4]{1,0:T(4,128)S(1)} copy-done((f32[4,4]{1,0:T(4,128)S(1)}, f32[4,4]{1,0:T(4,128)}, u32[]{:S(2)}) %copy-start.6) | copy-done | bytes 88
  7.3 53.6 %shard_map.82 = f32[128,1024]{1,0:T(8,128)S(1)} custom-call(f32[128,1024]{1,0:T(8,128)S(1)} %bitcast.3, f32[64,1024]{1,0:T(8,128)S(1)} %copy-done.2, f32[64,1024]{1,0:T(8,128)S(1)} %copy-done.3, f32[64,1024]{1,0:T(8,128)S(1)} %copy-done.4, f32[4,4]{1,0:T(4,128)S(1)} %copy-done.6, f32[4]{0:T(128)S(1)} %copy-done.7, f32[64,8,128]{2,1,0:T(8,128)S(1)} %copy-done.5, ...), custom_call_target="tpu_custom_call" | custom-call | tf_op jit(solution)/shard_map/pallas_call | solution.py:523
  61.0 0.8 %copy.10 = f32[1,2,64,1024]{3,2,1,0:T(8,128)} copy(f32[1,2,64,1024]{3,2,1,0:T(8,128)S(1)} %bitcast.2) | data formatting | bytes 1048576
Async XLA Ops:
  0.0 0.7 %copy-start.7 = (f32[4]{0:T(128)S(1)}, f32[4]{0:T(128)}, u32[]{:S(2)}) copy-start(f32[4]{0:T(128)} %gust.1) | copy-start | bytes 52
  0.7 1.1 %copy-start = (f32[8,192,128]{2,1,0:T(8,128)S(1)}, f32[8,192,128]{2,1,0:T(8,128)}, u32[]{:S(2)}) copy-start(f32[8,192,128]{2,1,0:T(8,128)} %constant.5.clone.cos_y) | copy-start | bytes 2359300
  1.8 1.0 %copy-start.1 = (f32[1,2,64,1024]{3,2,1,0:T(8,128)S(1)}, f32[1,2,64,1024]{3,2,1,0:T(8,128)}, u32[]{:S(2)}) copy-start(f32[1,2,64,1024]{3,2,1,0:T(8,128)} %param.8) | copy-start | bytes 1572868
  2.8 0.9 %copy-start.2 = (f32[64,1024]{1,0:T(8,128)S(1)}, f32[64,1024]{1,0:T(8,128)}, u32[]{:S(2)}) copy-start(f32[64,1024]{1,0:T(8,128)} %rigidity.1) | copy-start | bytes 786436
  3.8 0.9 %copy-start.3 = (f32[64,1024]{1,0:T(8,128)S(1)}, f32[64,1024]{1,0:T(8,128)}, u32[]{:S(2)}) copy-start(f32[64,1024]{1,0:T(8,128)} %inv_mass.1) | copy-start | bytes 786436
  4.7 0.9 %copy-start.4 = (f32[64,1024]{1,0:T(8,128)S(1)}, f32[64,1024]{1,0:T(8,128)}, u32[]{:S(2)}) copy-start(f32[64,1024]{1,0:T(8,128)} %gust_load.1) | copy-start | bytes 786436
  5.7 0.9 %copy-start.5 = (f32[64,8,128]{2,1,0:T(8,128)S(1)}, f32[64,8,128]{2,1,0:T(8,128)}, u32[]{:S(2)}) copy-start(f32[64,8,128]{2,1,0:T(8,128)} %constant.4.clone.cos_x) | copy-start | bytes 786436
  6.6 0.7 %copy-start.6 = (f32[4,4]{1,0:T(4,128)S(1)}, f32[4,4]{1,0:T(4,128)}, u32[]{:S(2)}) copy-start(f32[4,4]{1,0:T(4,128)} %kl_coeff.1) | copy-start | bytes 196

commit v2 on v1

v2 whole, which is shorter than its diff:
```python
import functools

import jax
import jax.numpy as jnp
import numpy as np
from jax import lax
from jax.experimental import pallas as pl
from jax.experimental.pallas import tpu as pltpu
from jax.sharding import PartitionSpec as P

FINE = 4
KL = 4
STIFF_SCALE = 1.0 / 64.0
TIME_STEP = 0.18
HALF_STEP = 0.09
DAMPING = 0.05
COARSE = FINE * TIME_STEP
KEEP = 1.0 - HALF_STEP * DAMPING
KEEP_COARSE = 1.0 - COARSE * DAMPING
RATIO = COARSE / HALF_STEP

HALO = 32
STRIP = 128
ROWS = 64
REGION = STRIP + 2 * HALO
PAD = 8
HALF = REGION // 2
CHUNK = 32
MESH = pl.DeviceIdType.MESH


def chunks(lo, hi):
    return [(a, min(a + CHUNK, hi)) for a in range(lo, hi, CHUNK)]


def kernel(
    tcount,
    scount,
    state,
    rigidity,
    inv_mass,
    gust_load,
    kl_coeff,
    gust,
    cos_x,
    cos_y,
    out,
    state_v,
    coef_v,
    cosx_v,
    cosy_v,
    turned,
    halo,
    coef_t,
    coef_h,
    got_core,
    got_mate,
    got_far,
    got_gust,
    coef_mate,
    coef_far,
    gust_row,
    stiff,
    kick,
    load,
    pos,
    vel,
    weighted,
    diff_p,
    diff_q,
    corr_p,
    corr_q,
    outgoing,
    incoming,
    result,
    local_sem,
    send_sem,
    recv_sem,
    coef_send,
    coef_recv,
    back_send,
    back_recv,
):
    t = lax.axis_index("tm")
    s = lax.axis_index("space")
    last = tcount - 1
    core = lax.rem(s, 2)
    mate = s + 1 - 2 * core
    far = s - 1 + 2 * core
    has_far = jnp.logical_and(far >= 0, far < scount)

    load_state = pltpu.make_async_copy(state, state_v, local_sem.at[0])
    load_state.start()
    loads = [
        pltpu.make_async_copy(src, dst, local_sem.at[1 + i])
        for i, (src, dst) in enumerate(
            [
                (rigidity, coef_v.at[0]),
                (inv_mass, coef_v.at[1]),
                (gust_load, coef_v.at[2]),
                (cos_x.at[s], cosx_v),
                (cos_y.at[t], cosy_v),
            ]
        )
    ]
    for copy in loads:
        copy.start()

    barrier = pltpu.get_barrier_semaphore()

    def greet(tt, ss):
        pl.semaphore_signal(barrier, inc=1, device_id=(tt, ss), device_id_type=MESH)

    for i in range(1, tcount):
        greet(lax.rem(t + i, tcount), s)
    greet(t, mate)

    @pl.when(has_far)
    def _():
        for i in range(tcount):
            greet(lax.rem(t + i, tcount), far)

    def lanes(rows):
        return lax.broadcasted_iota(jnp.int32, (rows, 128), 1)

    def remote(src, dst, send, recv, tt, ss):
        return pltpu.make_async_remote_copy(
            src_ref=src,
            dst_ref=dst,
            send_sem=send,
            recv_sem=recv,
            device_id=(tt, ss),
            device_id_type=MESH,
        )

    def strip_of(tt, rows):
        return pl.ds(pl.multiple_of(tt * STRIP, STRIP), rows)

    def core_copy(tt, slot):
        return remote(
            turned.at[strip_of(tt, REGION)], got_core.at[slot], send_sem.at[0, tt], recv_sem.at[0, slot], tt, s
        )

    def far_copy(tt, slot):
        return remote(
            halo.at[strip_of(tt, HALF)], got_far.at[slot], send_sem.at[1, tt], recv_sem.at[1, slot], tt, far
        )

    def mate_copy(slot):
        return remote(
            got_core.at[slot], got_mate.at[slot], send_sem.at[2, slot], recv_sem.at[2, slot], t, mate
        )

    def gust_copy(tt, slot):
        return remote(gust_row, got_gust.at[slot], send_sem.at[3, tt], recv_sem.at[3, slot], tt, s)

    coef_near = remote(coef_t, coef_mate, coef_send.at[0], coef_recv.at[0], t, mate)
    coef_away = remote(coef_h, coef_far, coef_send.at[1], coef_recv.at[1], t, far)
    own_copy = pltpu.make_async_copy(turned.at[strip_of(t, REGION)], got_core.at[t], local_sem.at[6])
    own_gust = pltpu.make_async_copy(gust_row, got_gust.at[t], local_sem.at[7])

    zero_halo = jnp.zeros((HALO, 128), jnp.float32)
    turned[0:HALO, :] = zero_halo
    turned[HALO + tcount * STRIP :, :] = zero_halo
    load_state.wait()
    for i in range(tcount):
        turned[HALO + i * STRIP : HALO + (i + 1) * STRIP, :] = state_v[
            :, i * STRIP : (i + 1) * STRIP
        ].T
    row8 = lax.broadcasted_iota(jnp.int32, (8, 128), 0)
    gust_block = jnp.zeros((8, 128), jnp.float32)
    for i in range(FINE):
        gust_block = jnp.where(row8 == i, gust[i], gust_block)
    gust_row[...] = gust_block

    def pack(near, further):
        upper = lax.rem(lanes(near.shape[0]), 64) >= 32
        return jnp.where(
            core == 0,
            jnp.where(upper, pltpu.roll(further, 32, 1), near),
            jnp.where(upper, near, pltpu.roll(further, 96, 1)),
        )

    for a, b in chunks(0, halo.shape[0]):
        halo[a:b, :] = pack(turned[a:b, :], turned[HALF + a : HALF + b, :])

    pl.semaphore_wait(barrier, tcount + tcount * has_far.astype(jnp.int32))

    def send_to(i):
        tt = lax.rem(t + i, tcount)
        if i < tcount:
            gust_copy(tt, t).start()

            @pl.when(t < last)
            def _():
                core_copy(tt, t).start()

        @pl.when(jnp.logical_and(t < last, has_far))
        def _():
            far_copy(tt, t).start()

    own_copy.start()
    own_gust.start()
    send_to(tcount)
    send_to(1)

    for copy in loads:
        copy.wait()

    def turn_coef(tile, first, rows, target):
        cols = pl.ds(pl.multiple_of(tile * STRIP, STRIP), STRIP)
        pair = jnp.concatenate([coef_v[0, :, cols], coef_v[1, :, cols]], axis=0).T
        other = jnp.concatenate([coef_v[2, :, cols], coef_v[2, :, cols]], axis=0).T
        coef_t[0, target : target + rows, :] = pair[first : first + rows]
        coef_t[1, target : target + rows, :] = other[first : first + rows]

    turn_coef(t, 0, STRIP, HALO)

    @pl.when(t > 0)
    def _():
        turn_coef(t - 1, STRIP - HALO, HALO, 0)

    @pl.when(t == 0)
    def _():
        coef_t[0, 0:HALO, :] = zero_halo
        coef_t[1, 0:HALO, :] = zero_halo

    @pl.when(t < last)
    def _():
        turn_coef(t + 1, 0, HALO, HALO + STRIP)

    @pl.when(t == last)
    def _():
        coef_t[0, HALO + STRIP :, :] = zero_halo
        coef_t[1, HALO + STRIP :, :] = zero_halo

    for k in range(2):
        coef_h[k] = pack(coef_t[k, 0:HALF, :], coef_t[k, HALF:, :])

    coef_near.start()

    @pl.when(has_far)
    def _():
        coef_away.start()

    for i in range(2, tcount):
        send_to(i)

    own_copy.wait()

    @pl.when(t < last)
    def _():
        mate_copy(t).start()

    @pl.when(jnp.logical_not(has_far))
    def _():
        coef_far[...] = jnp.zeros_like(coef_far)
        got_far[...] = jnp.zeros_like(got_far)

    mixed = []
    for b in range(KL):
        row = kl_coeff[0, b] * cosx_v[0:1, :]
        for a in range(1, KL):
            row = row + kl_coeff[a, b] * cosx_v[a : a + 1, :]
        mixed.append(row)
    mixed = jnp.concatenate(mixed + [jnp.zeros((128 - KL, 128), jnp.float32)], axis=0)
    field = jnp.dot(
        cosy_v[...], mixed, precision=lax.Precision.HIGHEST, preferred_element_type=jnp.float32
    )
    stiff[...] = STIFF_SCALE * jnp.exp(0.5 * jnp.tanh(field))

    zero_pad = jnp.zeros((PAD, 128), jnp.float32)
    for buf in (pos, weighted, corr_p, diff_p):
        for i in range(buf.shape[0]):
            buf[i, 0:PAD, :] = zero_pad
            buf[i, PAD + REGION :, :] = zero_pad

    def first_values(own, by_mate, by_far):
        lane = lanes(own.shape[0])
        from_mate = jnp.logical_and(lane >= 64 + 32 * core, lane < 96 + 32 * core)
        return jnp.where(lane < ROWS, own, jnp.where(from_mate, pltpu.roll(by_mate, 64, 1), by_far))

    def second_values(own, by_mate, by_far):
        lane = lanes(own.shape[0])
        from_mate = jnp.logical_and(lane >= 64 + 32 * core, lane < 96 + 32 * core)
        return jnp.where(lane < ROWS, pltpu.roll(own, 64, 1), jnp.where(from_mate, by_mate, by_far))

    def unpack(block, part):
        if part == 0:
            return pltpu.roll(block, 64, 1), block
        right, left = pltpu.roll(block, 32, 1), pltpu.roll(block, 96, 1)
        return jnp.where(core == 1, right, left), jnp.where(core == 1, left, right)

    coef_near.wait_recv()

    @pl.when(has_far)
    def _():
        coef_away.wait_recv()

    for part in range(2):
        for a, b in chunks(0, HALF):
            rows = slice(part * HALF + a, part * HALF + b)
            far_rig, far_mass = unpack(coef_far[0, a:b, :], part)
            far_load, _ = unpack(coef_far[1, a:b, :], part)
            rig = first_values(coef_t[0, rows, :], coef_mate[0, rows, :], far_rig)
            mass = HALF_STEP * second_values(coef_t[0, rows, :], coef_mate[0, rows, :], far_mass)
            stiff[rows, :] *= rig
            kick[0, rows, :] = mass
            kick[1, rows, :] = (1.0 + KEEP) * mass
            kick[2, rows, :] = RATIO * mass
            load[rows, :] = mass * first_values(coef_t[1, rows, :], coef_mate[1, rows, :], far_load)

    def laplace(ref, slot, a, b):
        centre = ref[slot, PAD + a : PAD + b, :]
        rows = ref[slot, PAD + a - 1 : PAD + b - 1, :] + ref[slot, PAD + a + 1 : PAD + b + 1, :]
        sides = pltpu.roll(centre, 1, 1) + pltpu.roll(centre, 127, 1)
        return (rows + sides) - 4.0 * centre

    def stencil(ref, slot, scratch, lo, finish):
        hi = REGION - lo
        ahead = chunks(max(lo - 8, 0), min(hi + 8, REGION))
        for a, b in chunks(lo, hi):
            while ahead and ahead[0][0] < b + 8:
                c, d = ahead.pop(0)
                weighted[scratch, PAD + c : PAD + d, :] = stiff[c:d, :] * laplace(ref, slot, c, d)
            finish(a, b, laplace(weighted, scratch, a, b))

    def fine_tail(slot, scratch, g, lows, finish):
        for i in range(1, FINE):
            push = KEEP * g[i - 1] + g[i]

            def move(a, b, spring, push=push):
                half = (
                    (KEEP * KEEP) * vel[slot, a:b, :] - kick[1, a:b, :] * spring + load[a:b, :] * push
                )
                pos[slot, PAD + a : PAD + b, :] += TIME_STEP * half
                vel[slot, a:b, :] = half

            stencil(pos, slot, scratch, lows[i], move)

        def close(a, b, spring):
            finish(
                a,
                b,
                pos[slot, PAD + a : PAD + b, :],
                KEEP * vel[slot, a:b, :] - kick[0, a:b, :] * spring + load[a:b, :] * g[FINE - 1],
            )

        stencil(pos, slot, scratch, lows[FINE], close)

    def gusts(n):
        return [got_gust[n, i : i + 1, :] for i in range(FINE)]

    def forward(i):
        n = lax.rem(t - i + tcount, tcount)

        @pl.when(n < last)
        def _():
            core_copy(n, n).wait_recv()
            mate_copy(n).start()

    forward(1)

    def first_sweep(i, carry):
        n = lax.rem(t - i + tcount, tcount)

        @pl.when(jnp.logical_and(i > 0, i < last))
        def _():
            forward(i + 1)

        @pl.when(i > 0)
        def _():
            gust_copy(n, n).wait_recv()

        @pl.when(i == 0)
        def _():
            own_gust.wait()

        @pl.when(jnp.logical_and(has_far, n < last))
        def _():
            far_copy(n, n).wait_recv()

        @pl.when(n < last)
        def _():
            mate_copy(n).wait_recv()
            for part in range(2):
                for a, b in chunks(0, HALF):
                    c, d = part * HALF + a, part * HALF + b
                    p_far, q_far = unpack(got_far[n, a:b, :], part)
                    own = got_core[n, c:d, :]
                    other = got_mate[n, c:d, :]
                    pos[0, PAD + c : PAD + d, :] = first_values(own, other, p_far)
                    vel[0, c:d, :] = second_values(own, other, q_far)
            share = jnp.where(n > 0, 1.0, 0.0)
            g = gusts(n)

            def begin(a, b, spring):
                p = pos[0, PAD + a : PAD + b, :]
                q = vel[0, a:b, :]
                coarse_q = KEEP_COARSE * q - kick[2, a:b, :] * spring
                diff_q[n, a:b, :] = -share * coarse_q
                diff_p[n, PAD + a : PAD + b, :] = -share * (p + COARSE * coarse_q)
                half = KEEP * q - kick[0, a:b, :] * spring + load[a:b, :] * g[0]
                pos[0, PAD + a : PAD + b, :] = p + TIME_STEP * half
                vel[0, a:b, :] = half

            def end(a, b, new_p, new_q):
                diff_p[n, PAD + a : PAD + b, :] += new_p
                diff_q[n, a:b, :] += new_q

            stencil(pos, 0, 0, 0, begin)
            fine_tail(0, 0, g, (0, 0, 0, 8, 8), end)

        return carry

    lax.fori_loop(0, tcount, first_sweep, 0)

    def back_copy(n, slot):
        return remote(outgoing.at[n], incoming.at[slot], back_send.at[n], back_recv.at[slot], n, s)

    def stage(n, a, b, p, q):
        first, end = max(a, HALO), min(b, HALO + STRIP)
        if first < end:
            outgoing[n, first - HALO : end - HALO, :] = jnp.where(
                lanes(end - first) < ROWS,
                p[first - a : end - a],
                pltpu.roll(q[first - a : end - a], 64, 1),
            )

    def send_back(n):
        @pl.when(t != n)
        def _():
            back_copy(n, t).start()

    for a, b in chunks(HALO, HALO + STRIP):
        stage(0, a, b, diff_p[0, PAD + a : PAD + b, :], diff_q[0, a:b, :])
    send_back(0)

    for n in range(1, tcount):
        slot = n % 2
        lows = [(10 + 2 * n + 2 * k) // 8 * 8 for k in range(FINE + 1)]
        g = gusts(n)

        def begin(a, b, spring, n=n, slot=slot, g=g):
            p = diff_p[n - 1, PAD + a : PAD + b, :]
            q = diff_q[n - 1, a:b, :]
            if n < last:
                coarse_q = KEEP_COARSE * q - kick[2, a:b, :] * spring
                diff_q[n, a:b, :] += coarse_q
                diff_p[n, PAD + a : PAD + b, :] += p + COARSE * coarse_q
            half = KEEP * q - kick[0, a:b, :] * spring + load[a:b, :] * g[0]
            pos[slot, PAD + a : PAD + b, :] = p + TIME_STEP * half
            vel[slot, a:b, :] = half

        stencil(diff_p, n - 1, 2 + slot, lows[0], begin)

        if n > 1:

            def correct(a, b, spring, slot=slot):
                coarse_q = KEEP_COARSE * corr_q[slot, a:b, :] - kick[2, a:b, :] * spring
                corr_q[slot, a:b, :] = coarse_q
                corr_p[slot, PAD + a : PAD + b, :] += COARSE * coarse_q

            stencil(corr_p, slot, 4, lows[FINE], correct)

        def end(a, b, new_p, new_q, n=n, slot=slot):
            if n > 1:
                new_p = new_p + corr_p[slot, PAD + a : PAD + b, :]
                new_q = new_q + corr_q[slot, a:b, :]
            if n < last:
                corr_p[1 - slot, PAD + a : PAD + b, :] = new_p - diff_p[n, PAD + a : PAD + b, :]
                corr_q[1 - slot, a:b, :] = new_q - diff_q[n, a:b, :]
            stage(n, a, b, new_p, new_q)

        fine_tail(slot, slot, g, lows, end)
        send_back(n)

    def place(tt, block):
        cols = pl.ds(pl.multiple_of(tt * STRIP, STRIP), STRIP)
        result[:, cols] = block.T

    place(t, outgoing[t])
    for i in range(1, tcount):
        tt = lax.rem(t + i, tcount)
        back_copy(tt, tt).wait_recv()
        place(tt, incoming[tt])
    store = pltpu.make_async_copy(result, out, local_sem.at[0])
    store.start()

    for i in range(1, tcount + 1):
        tt = lax.rem(t + i, tcount)
        if i < tcount:
            back_copy(tt, t).wait_send()
            gust_copy(tt, t).wait_send()

            @pl.when(t < last)
            def _():
                core_copy(tt, t).wait_send()

        @pl.when(tt < last)
        def _():
            mate_copy(tt).wait_send()

        @pl.when(jnp.logical_and(t < last, has_far))
        def _():
            far_copy(tt, t).wait_send()

    coef_near.wait_send()

    @pl.when(has_far)
    def _():
        coef_away.wait_send()

    store.wait()


def tables(tcount, scount, rows, cols):
    orders = np.arange(1, KL + 1)
    lane = np.arange(128)
    along = np.where(lane < ROWS + HALO, lane, lane - 128)
    x = np.arange(scount)[:, None] * ROWS + along[None, :]
    y = np.arange(tcount)[:, None] * STRIP - HALO + np.arange(REGION)[None, :]
    cos_x = np.zeros((scount, 8, 128), np.float32)
    cos_x[:, :KL] = np.cos(np.pi * orders[None, :, None] * ((x[:, None, :] + 0.5) / rows))
    cos_y = np.zeros((tcount, REGION, 128), np.float32)
    cos_y[:, :, :KL] = np.cos(np.pi * orders[None, None, :] * ((y[:, :, None] + 0.5) / cols))
    return cos_x, cos_y


def per_device(tcount, scount, start_state, rigidity, inv_mass, gust_load, kl_coeff, gust_history):
    rows, cols = rigidity.shape
    cos_x, cos_y = tables(tcount, scount, rows * scount, cols)
    f32 = jnp.float32
    padded = PAD + REGION + PAD
    packed = (tcount - 1) * STRIP + HALF
    vmem = pltpu.VMEM
    dma = pltpu.SemaphoreType.DMA
    hbm = pl.BlockSpec(memory_space=pltpu.HBM)
    scalars = pl.BlockSpec(memory_space=pltpu.SMEM)
    result = pl.pallas_call(
        functools.partial(kernel, tcount, scount),
        out_shape=jax.ShapeDtypeStruct((2 * rows, cols), f32),
        in_specs=[hbm] * 4 + [scalars] * 2 + [hbm] * 2,
        out_specs=hbm,
        scratch_shapes=[
            vmem((2 * rows, cols), f32),
            vmem((3, rows, cols), f32),
            vmem((8, 128), f32),
            vmem((REGION, 128), f32),
            vmem((2 * HALO + tcount * STRIP, 128), f32),
            vmem((packed, 128), f32),
            vmem((2, REGION, 128), f32),
            vmem((2, HALF, 128), f32),
            vmem((tcount, REGION, 128), f32),
            vmem((tcount, REGION, 128), f32),
            vmem((tcount, HALF, 128), f32),
            vmem((tcount, 8, 128), f32),
            vmem((2, REGION, 128), f32),
            vmem((2, HALF, 128), f32),
            vmem((8, 128), f32),
            vmem((REGION, 128), f32),
            vmem((3, REGION, 128), f32),
            vmem((REGION, 128), f32),
            vmem((2, padded, 128), f32),
            vmem((2, REGION, 128), f32),
            vmem((5, padded, 128), f32),
            vmem((tcount - 1, padded, 128), f32),
            vmem((tcount - 1, REGION, 128), f32),
            vmem((2, padded, 128), f32),
            vmem((2, REGION, 128), f32),
            vmem((tcount, STRIP, 128), f32),
            vmem((tcount, STRIP, 128), f32),
            vmem((2 * rows, cols), f32),
            dma((8,)),
            dma((4, tcount)),
            dma((4, tcount)),
            dma((2,)),
            dma((2,)),
            dma((tcount,)),
            dma((tcount,)),
        ],
        compiler_params=pltpu.CompilerParams(
            collective_id=0, has_side_effects=True, vmem_limit_bytes=60 * 1024 * 1024
        ),
    )(
        start_state.reshape(2 * rows, cols),
        rigidity,
        inv_mass,
        gust_load,
        kl_coeff,
        gust_history,
        jnp.asarray(cos_x),
        jnp.asarray(cos_y),
    )
    return result.reshape(1, 2, rows, cols)


def solution(mesh):
    in_specs = (
        P("tm", None, "space", None),
        P("space", None),
        P("space", None),
        P("space", None),
        P(),
        P("tm"),
    )
    return jax.shard_map(
        functools.partial(per_device, mesh.shape["tm"], mesh.shape["space"]),
        mesh=mesh,
        in_specs=in_specs,
        out_specs=P("tm", None, "space", None),
        check_vma=False,
    )
```

time: 62.1 us -> 51 us (0.82)
  local copies, waits for them, and re-layouts: 8.1 us -> 1.89 us
  Pallas kernels: 53.6 us -> 48.2 us
    unnamed x17 -> x1, local copies, waits for them, and re-layouts: 8.1 us -> 1.89 us
    pallas_call x1, Pallas kernels: 53.6 us -> 48.2 us  [per_device(): pl.pallas_call(functools.partial(kernel, tcount, scount), out_shape=jax.S...]
where the time goes in v2:
time: 51 us; the launch traced here: 50.1 us
  Pallas kernels  48.2 us (95%)
  local copies, waits for them, and re-layouts  1.89 us (4%)
    pallas_call x1, Pallas kernels, per_device(): pl.pallas_call(functools.partial(kernel, tcount, scount), out_shape=jax.S...  48.2 us
    unnamed x1, local copies, waits for them, and re-layouts  1.89 us

profile of v2, /device:TPU:7, one launch (start us, length us, event | category | flops | bytes accessed | tf_op | source)
XLA Modules:
  0.0 50.1 jit_solution(12081464267472360854)
XLA Ops:
  0.0 48.2 %shard_map.82 = f32[128,1024]{1,0:T(8,128)} custom-call(f32[128,1024]{1,0:T(8,128)} %bitcast.3, f32[64,1024]{1,0:T(8,128)} %rigidity.1, f32[64,1024]{1,0:T(8,128)} %inv_mass.1, f32[64,1024]{1,0:T(8,128)} %gust_load.1, f32[4,4]{1,0:T(4,128)} %kl_coeff.1, f32[4]{0:T(128)} %gust.1, f32[64,8,128]{2,1,0:T(8,128)} %constant.4.clone.cos_x, ...), custom_call_target="tpu_custom_call" | custom-call | tf_op jit(solution)/shard_map/pallas_call | solution.py:540
  48.2 1.9 %copy.10 = f32[1,2,64,1024]{3,2,1,0:T(8,128)} copy(f32[1,2,64,1024]{3,2,1,0:T(8,128)} %bitcast.2) | data formatting | bytes 1048576

commit v3 on v2

--- a/solution.py
+++ b/solution.py
@@ -47,6 +47,8 @@
     out,
     state_v,
     coef_v,
+    kl_v,
+    gust_v,
     cosx_v,
     cosy_v,
     turned,
@@ -72,7 +74,6 @@
     corr_q,
     outgoing,
     incoming,
-    result,
     local_sem,
     send_sem,
     recv_sem,
@@ -91,6 +92,8 @@
 
     load_state = pltpu.make_async_copy(state, state_v, local_sem.at[0])
     load_state.start()
+    load_gust = pltpu.make_async_copy(gust, gust_v, local_sem.at[9])
+    load_gust.start()
     loads = [
         pltpu.make_async_copy(src, dst, local_sem.at[1 + i])
         for i, (src, dst) in enumerate(
@@ -100,6 +103,7 @@
                 (gust_load, coef_v.at[2]),
                 (cos_x.at[s], cosx_v),
                 (cos_y.at[t], cosy_v),
+                (kl_coeff, kl_v),
             ]
         )
     ]
@@ -156,13 +160,14 @@
 
     coef_near = remote(coef_t, coef_mate, coef_send.at[0], coef_recv.at[0], t, mate)
     coef_away = remote(coef_h, coef_far, coef_send.at[1], coef_recv.at[1], t, far)
-    own_copy = pltpu.make_async_copy(turned.at[strip_of(t, REGION)], got_core.at[t], local_sem.at[6])
-    own_gust = pltpu.make_async_copy(gust_row, got_gust.at[t], local_sem.at[7])
+    own_copy = pltpu.make_async_copy(turned.at[strip_of(t, REGION)], got_core.at[t], local_sem.at[7])
+    own_gust = pltpu.make_async_copy(gust_row, got_gust.at[t], local_sem.at[8])
 
     zero_halo = jnp.zeros((HALO, 128), jnp.float32)
     turned[0:HALO, :] = zero_halo
     turned[HALO + tcount * STRIP :, :] = zero_halo
     load_state.wait()
+    load_gust.wait()
     for i in range(tcount):
         turned[HALO + i * STRIP : HALO + (i + 1) * STRIP, :] = state_v[
             :, i * STRIP : (i + 1) * STRIP
@@ -170,7 +175,7 @@
     row8 = lax.broadcasted_iota(jnp.int32, (8, 128), 0)
     gust_block = jnp.zeros((8, 128), jnp.float32)
     for i in range(FINE):
-        gust_block = jnp.where(row8 == i, gust[i], gust_block)
+        gust_block = jnp.where(row8 == i, gust_v[0:1, i : i + 1], gust_block)
     gust_row[...] = gust_block
 
     def pack(near, further):
@@ -259,9 +264,9 @@
 
     mixed = []
     for b in range(KL):
-        row = kl_coeff[0, b] * cosx_v[0:1, :]
+        row = kl_v[0:1, b : b + 1] * cosx_v[0:1, :]
         for a in range(1, KL):
-            row = row + kl_coeff[a, b] * cosx_v[a : a + 1, :]
+            row = row + kl_v[a : a + 1, b : b + 1] * cosx_v[a : a + 1, :]
         mixed.append(row)
     mixed = jnp.concatenate(mixed + [jnp.zeros((128 - KL, 128), jnp.float32)], axis=0)
     field = jnp.dot(
@@ -316,104 +321,125 @@
         sides = pltpu.roll(centre, 1, 1) + pltpu.roll(centre, 127, 1)
         return (rows + sides) - 4.0 * centre
 
-    def stencil(ref, slot, scratch, lo, finish):
-        hi = REGION - lo
-        ahead = chunks(max(lo - 8, 0), min(hi + 8, REGION))
-        for a, b in chunks(lo, hi):
-            while ahead and ahead[0][0] < b + 8:
-                c, d = ahead.pop(0)
-                weighted[scratch, PAD + c : PAD + d, :] = stiff[c:d, :] * laplace(ref, slot, c, d)
-            finish(a, b, laplace(weighted, scratch, a, b))
-
-    def fine_tail(slot, scratch, g, lows, finish):
-        for i in range(1, FINE):
-            push = KEEP * g[i - 1] + g[i]
-
-            def move(a, b, spring, push=push):
-                half = (
-                    (KEEP * KEEP) * vel[slot, a:b, :] - kick[1, a:b, :] * spring + load[a:b, :] * push
-                )
-                pos[slot, PAD + a : PAD + b, :] += TIME_STEP * half
-                vel[slot, a:b, :] = half
-
-            stencil(pos, slot, scratch, lows[i], move)
-
-        def close(a, b, spring):
-            finish(
+    def stencils(work):
+        spans = [chunks(max(lo - 8, 0), min(REGION - lo + 8, REGION)) for _, _, lo, _ in work]
+        for k in range(max(map(len, spans))):
+            for w, (ref, slot, _, _) in enumerate(work):
+                if k < len(spans[w]):
+                    a, b = spans[w][k]
+                    weighted[w, PAD + a : PAD + b, :] = stiff[a:b, :] * laplace(ref, slot, a, b)
+        spans = [chunks(lo, REGION - lo) for _, _, lo, _ in work]
+        for k in range(max(map(len, spans))):
+            for w, (_, _, _, finish) in enumerate(work):
+                if k < len(spans[w]):
+                    a, b = spans[w][k]
+                    finish(a, b, laplace(weighted, w, a, b))
+
+    def move(slot, g, i):
+        push = KEEP * g[i - 1] + g[i]
+
+        def finish(a, b, spring):
+            half = (KEEP * KEEP) * vel[slot, a:b, :] - kick[1, a:b, :] * spring + load[a:b, :] * push
+            pos[slot, PAD + a : PAD + b, :] += TIME_STEP * half
+            vel[slot, a:b, :] = half
+
+        return finish
+
+    def close(slot, g, end):
+        def finish(a, b, spring):
+            end(
                 a,
                 b,
                 pos[slot, PAD + a : PAD + b, :],
                 KEEP * vel[slot, a:b, :] - kick[0, a:b, :] * spring + load[a:b, :] * g[FINE - 1],
             )
 
-        stencil(pos, slot, scratch, lows[FINE], close)
+        return finish
 
     def gusts(n):
         return [got_gust[n, i : i + 1, :] for i in range(FINE)]
 
-    def forward(i):
-        n = lax.rem(t - i + tcount, tcount)
-
-        @pl.when(n < last)
+    def nth(i):
+        return lax.rem(t - i + 2 * last, last)
+
+    def forward(n):
+        @pl.when(n != t)
         def _():
             core_copy(n, n).wait_recv()
             mate_copy(n).start()
 
-    forward(1)
-
-    def first_sweep(i, carry):
-        n = lax.rem(t - i + tcount, tcount)
-
-        @pl.when(jnp.logical_and(i > 0, i < last))
-        def _():
-            forward(i + 1)
-
-        @pl.when(i > 0)
+    def receive(slot, n):
+        @pl.when(n != t)
         def _():
             gust_copy(n, n).wait_recv()
 
-        @pl.when(i == 0)
-        def _():
-            own_gust.wait()
-
-        @pl.when(jnp.logical_and(has_far, n < last))
+        @pl.when(has_far)
         def _():
             far_copy(n, n).wait_recv()
 
-        @pl.when(n < last)
-        def _():
-            mate_copy(n).wait_recv()
-            for part in range(2):
-                for a, b in chunks(0, HALF):
-                    c, d = part * HALF + a, part * HALF + b
-                    p_far, q_far = unpack(got_far[n, a:b, :], part)
-                    own = got_core[n, c:d, :]
-                    other = got_mate[n, c:d, :]
-                    pos[0, PAD + c : PAD + d, :] = first_values(own, other, p_far)
-                    vel[0, c:d, :] = second_values(own, other, q_far)
+        mate_copy(n).wait_recv()
+        for part in range(2):
+            for a, b in chunks(0, HALF):
+                c, d = part * HALF + a, part * HALF + b
+                p_far, q_far = unpack(got_far[n, a:b, :], part)
+                own = got_core[n, c:d, :]
+                other = got_mate[n, c:d, :]
+                pos[slot, PAD + c : PAD + d, :] = first_values(own, other, p_far)
+                vel[slot, c:d, :] = second_values(own, other, q_far)
+
+    def first_sweep(slices):
+        def begin(slot, n, g):
             share = jnp.where(n > 0, 1.0, 0.0)
-            g = gusts(n)
-
-            def begin(a, b, spring):
-                p = pos[0, PAD + a : PAD + b, :]
-                q = vel[0, a:b, :]
+
+            def finish(a, b, spring):
+                p = pos[slot, PAD + a : PAD + b, :]
+                q = vel[slot, a:b, :]
                 coarse_q = KEEP_COARSE * q - kick[2, a:b, :] * spring
                 diff_q[n, a:b, :] = -share * coarse_q
                 diff_p[n, PAD + a : PAD + b, :] = -share * (p + COARSE * coarse_q)
                 half = KEEP * q - kick[0, a:b, :] * spring + load[a:b, :] * g[0]
-                pos[0, PAD + a : PAD + b, :] = p + TIME_STEP * half
-                vel[0, a:b, :] = half
-
-            def end(a, b, new_p, new_q):
+                pos[slot, PAD + a : PAD + b, :] = p + TIME_STEP * half
+                vel[slot, a:b, :] = half
+
+            return finish
+
+        def end(n):
+            def finish(a, b, new_p, new_q):
                 diff_p[n, PAD + a : PAD + b, :] += new_p
                 diff_q[n, a:b, :] += new_q
 
-            stencil(pos, 0, 0, 0, begin)
-            fine_tail(0, 0, g, (0, 0, 0, 8, 8), end)
-
+            return finish
+
+        for slot, n in enumerate(slices):
+            receive(slot, n)
+        todo = [(slot, n, gusts(n)) for slot, n in enumerate(slices)]
+        stencils([(pos, slot, 0, begin(slot, n, g)) for slot, n, g in todo])
+        for i in range(1, FINE):
+            stencils([(pos, slot, 0 if i < 3 else 8, move(slot, g, i)) for slot, n, g in todo])
+        stencils([(pos, slot, 8, close(slot, g, end(n))) for slot, n, g in todo])
+
+    own_gust.wait()
+    forward(nth(0))
+    forward(nth(1))
+    forward(nth(2))
+    first_sweep([nth(0)])
+
+    def pair(k, carry):
+        i = 2 * k + 1
+
+        @pl.when(k < (last - 1) // 2 - 1)
+        def _():
+            forward(nth(i + 2))
+            forward(nth(i + 3))
+
+        first_sweep([nth(i), nth(i + 1)])
         return carry
 
-    lax.fori_loop(0, tcount, first_sweep, 0)
+    lax.fori_loop(0, (last - 1) // 2, pair, 0)
+
+    @pl.when(t != last)
+    def _():
+        gust_copy(last, last).wait_recv()
 
     def back_copy(n, slot):
         return remote(outgoing.at[n], incoming.at[slot], back_send.at[n], back_recv.at[slot], n, s)
@@ -436,12 +462,12 @@
         stage(0, a, b, diff_p[0, PAD + a : PAD + b, :], diff_q[0, a:b, :])
     send_back(0)
 
-    for n in range(1, tcount):
-        slot = n % 2
-        lows = [(10 + 2 * n + 2 * k) // 8 * 8 for k in range(FINE + 1)]
+    lows = {n: [(10 + 2 * n + 2 * k) // 8 * 8 for k in range(FINE + 1)] for n in range(1, tcount)}
+
+    def begin(n):
         g = gusts(n)
 
-        def begin(a, b, spring, n=n, slot=slot, g=g):
+        def finish(a, b, spring):
             p = diff_p[n - 1, PAD + a : PAD + b, :]
             q = diff_q[n - 1, a:b, :]
             if n < last:
@@ -449,21 +475,23 @@
                 diff_q[n, a:b, :] += coarse_q
                 diff_p[n, PAD + a : PAD + b, :] += p + COARSE * coarse_q
             half = KEEP * q - kick[0, a:b, :] * spring + load[a:b, :] * g[0]
-            pos[slot, PAD + a : PAD + b, :] = p + TIME_STEP * half
-            vel[slot, a:b, :] = half
-
-        stencil(diff_p, n - 1, 2 + slot, lows[0], begin)
-
-        if n > 1:
-
-            def correct(a, b, spring, slot=slot):
-                coarse_q = KEEP_COARSE * corr_q[slot, a:b, :] - kick[2, a:b, :] * spring
-                corr_q[slot, a:b, :] = coarse_q
-                corr_p[slot, PAD + a : PAD + b, :] += COARSE * coarse_q
-
-            stencil(corr_p, slot, 4, lows[FINE], correct)
-
-        def end(a, b, new_p, new_q, n=n, slot=slot):
+            pos[n, PAD + a : PAD + b, :] = p + TIME_STEP * half
+            vel[n, a:b, :] = half
+
+        return finish
+
+    def correct(slot):
+        def finish(a, b, spring):
+            coarse_q = KEEP_COARSE * corr_q[slot, a:b, :] - kick[2, a:b, :] * spring
+            corr_q[slot, a:b, :] = coarse_q
+            corr_p[slot, PAD + a : PAD + b, :] += COARSE * coarse_q
+
+        return finish
+
+    def end(n):
+        slot = n % 2
+
+        def finish(a, b, new_p, new_q):
             if n > 1:
                 new_p = new_p + corr_p[slot, PAD + a : PAD + b, :]
                 new_q = new_q + corr_q[slot, a:b, :]
@@ -472,20 +500,34 @@
                 corr_q[1 - slot, a:b, :] = new_q - diff_q[n, a:b, :]
             stage(n, a, b, new_p, new_q)
 
-        fine_tail(slot, slot, g, lows, end)
-        send_back(n)
+        return finish
+
+    for turn in range(1, tcount + FINE):
+        work = []
+        if turn < tcount:
+            work.append((diff_p, turn - 1, lows[turn][0], begin(turn)))
+        for i in range(1, FINE):
+            n = turn - i
+            if 1 <= n < tcount:
+                work.append((pos, n, lows[n][i], move(n, gusts(n), i)))
+        n = turn - FINE
+        if n >= 1:
+            if n > 1:
+                work.append((corr_p, n % 2, lows[n][FINE], correct(n % 2)))
+            work.append((pos, n, lows[n][FINE], close(n, gusts(n), end(n))))
+        stencils(work)
+        if n >= 1:
+            send_back(n)
 
     def place(tt, block):
         cols = pl.ds(pl.multiple_of(tt * STRIP, STRIP), STRIP)
-        result[:, cols] = block.T
+        out[:, cols] = block.T
 
     place(t, outgoing[t])
     for i in range(1, tcount):
         tt = lax.rem(t + i, tcount)
         back_copy(tt, tt).wait_recv()
         place(tt, incoming[tt])
-    store = pltpu.make_async_copy(result, out, local_sem.at[0])
-    store.start()
 
     for i in range(1, tcount + 1):
         tt = lax.rem(t + i, tcount)
@@ -510,8 +552,6 @@
     @pl.when(has_far)
     def _():
         coef_away.wait_send()
-
-    store.wait()
 
 
 def tables(tcount, scount, rows, cols):
@@ -536,15 +576,16 @@
     vmem = pltpu.VMEM
     dma = pltpu.SemaphoreType.DMA
     hbm = pl.BlockSpec(memory_space=pltpu.HBM)
-    scalars = pl.BlockSpec(memory_space=pltpu.SMEM)
     result = pl.pallas_call(
         functools.partial(kernel, tcount, scount),
-        out_shape=jax.ShapeDtypeStruct((2 * rows, cols), f32),
-        in_specs=[hbm] * 4 + [scalars] * 2 + [hbm] * 2,
-        out_specs=hbm,
+        out_shape=pltpu.VMEM((2 * rows, cols), f32),
+        in_specs=[hbm] * 8,
+        out_specs=pl.BlockSpec(memory_space=pltpu.VMEM),
         scratch_shapes=[
             vmem((2 * rows, cols), f32),
             vmem((3, rows, cols), f32),
+            vmem((KL, KL), f32),
+            vmem((1, FINE), f32),
             vmem((8, 128), f32),
             vmem((REGION, 128), f32),
             vmem((2 * HALO + tcount * STRIP, 128), f32),
@@ -561,17 +602,16 @@
             vmem((REGION, 128), f32),
             vmem((3, REGION, 128), f32),
             vmem((REGION, 128), f32),
-            vmem((2, padded, 128), f32),
-            vmem((2, REGION, 128), f32),
-            vmem((5, padded, 128), f32),
+            vmem((tcount, padded, 128), f32),
+            vmem((tcount, REGION, 128), f32),
+            vmem((6, padded, 128), f32),
             vmem((tcount - 1, padded, 128), f32),
             vmem((tcount - 1, REGION, 128), f32),
             vmem((2, padded, 128), f32),
             vmem((2, REGION, 128), f32),
             vmem((tcount, STRIP, 128), f32),
             vmem((tcount, STRIP, 128), f32),
-            vmem((2 * rows, cols), f32),
-            dma((8,)),
+            dma((10,)),
             dma((4, tcount)),
             dma((4, tcount)),
             dma((2,)),
@@ -588,7 +628,7 @@
         inv_mass,
         gust_load,
         kl_coeff,
-        gust_history,
+        gust_history.reshape(1, FINE),
         jnp.asarray(cos_x),
         jnp.asarray(cos_y),
     )

time: 51 us -> 45.6 us (0.89)
  Pallas kernels: 48.2 us -> 44 us
  local copies, waits for them, and re-layouts: 1.89 us -> 0.8 us
    pallas_call x1, Pallas kernels: 48.2 us -> 44 us  [per_device(): pl.pallas_call(functools.partial(kernel, tcount, scount), out_shape=pltpu...]
    unnamed x1, local copies, waits for them, and re-layouts: 1.89 us -> 0.8 us
where the time goes in v3:
time: 45.6 us; the launch traced here: 44.8 us
  Pallas kernels  44 us (96%)
  local copies, waits for them, and re-layouts  0.8 us (2%)
    pallas_call x1, Pallas kernels, per_device(): pl.pallas_call(functools.partial(kernel, tcount, scount), out_shape=pltpu...  44 us

profile of v3, /device:TPU:7, one launch (start us, length us, event | category | flops | bytes accessed | tf_op | source)
XLA Modules:
  0.0 44.8 jit_solution(15553445860325793143)
XLA Ops:
  0.0 44.0 %shard_map.82 = f32[128,1024]{1,0:T(8,128)S(1)} custom-call(f32[128,1024]{1,0:T(8,128)} %bitcast.4, f32[64,1024]{1,0:T(8,128)} %rigidity.1, f32[64,1024]{1,0:T(8,128)} %inv_mass.1, f32[64,1024]{1,0:T(8,128)} %gust_load.1, f32[4,4]{1,0:T(4,128)} %kl_coeff.1, f32[1,4]{1,0:T(1,128)} %bitcast.5, f32[64,8,128]{2,1,0:T(8,128)} %constant.4.clone.cos_x, ...), custom_call_target="tpu_custom_call" | custom-call | tf_op jit(solution)/shard_map/pallas_call | solution.py:579
  44.0 0.8 %copy.10 = f32[1,2,64,1024]{3,2,1,0:T(8,128)} copy(f32[1,2,64,1024]{3,2,1,0:T(8,128)S(1)} %bitcast.3) | data formatting | bytes 1048576

commit v4 on v3

--- a/solution.py
+++ b/solution.py
@@ -72,6 +72,12 @@
     diff_q,
     corr_p,
     corr_q,
+    chain_p,
+    chain_q,
+    closed,
+    history,
+    kept_p,
+    kept_q,
     outgoing,
     incoming,
     local_sem,
@@ -124,6 +130,9 @@
         for i in range(tcount):
             greet(lax.rem(t + i, tcount), far)
 
+    def reversed_bits(i):
+        return i % 2 * 4 + i // 2 % 2 * 2 + i // 4
+
     def lanes(rows):
         return lax.broadcasted_iota(jnp.int32, (rows, 128), 1)
 
@@ -192,8 +201,8 @@
     pl.semaphore_wait(barrier, tcount + tcount * has_far.astype(jnp.int32))
 
     def send_to(i):
-        tt = lax.rem(t + i, tcount)
-        if i < tcount:
+        tt = lax.rem(t + reversed_bits(i), tcount)
+        if i > 0:
             gust_copy(tt, t).start()
 
             @pl.when(t < last)
@@ -206,7 +215,7 @@
 
     own_copy.start()
     own_gust.start()
-    send_to(tcount)
+    send_to(0)
     send_to(1)
 
     for copy in loads:
@@ -335,13 +344,13 @@
                     a, b = spans[w][k]
                     finish(a, b, laplace(weighted, w, a, b))
 
-    def move(slot, g, i):
+    def move(slot, target, g, i):
         push = KEEP * g[i - 1] + g[i]
 
         def finish(a, b, spring):
             half = (KEEP * KEEP) * vel[slot, a:b, :] - kick[1, a:b, :] * spring + load[a:b, :] * push
-            pos[slot, PAD + a : PAD + b, :] += TIME_STEP * half
-            vel[slot, a:b, :] = half
+            pos[target, PAD + a : PAD + b, :] = pos[slot, PAD + a : PAD + b, :] + TIME_STEP * half
+            vel[target, a:b, :] = half
 
         return finish
 
@@ -360,7 +369,9 @@
         return [got_gust[n, i : i + 1, :] for i in range(FINE)]
 
     def nth(i):
-        return lax.rem(t - i + 2 * last, last)
+        skipped = reversed_bits(lax.rem(t + 1, tcount))
+        place_in_order = i + jnp.where(i >= skipped, 1, 0)
+        return lax.rem(t - reversed_bits(place_in_order) + tcount, tcount)
 
     def forward(n):
         @pl.when(n != t)
@@ -395,18 +406,18 @@
                 p = pos[slot, PAD + a : PAD + b, :]
                 q = vel[slot, a:b, :]
                 coarse_q = KEEP_COARSE * q - kick[2, a:b, :] * spring
-                diff_q[n, a:b, :] = -share * coarse_q
-                diff_p[n, PAD + a : PAD + b, :] = -share * (p + COARSE * coarse_q)
+                kept_q[slot, a:b, :] = -share * coarse_q
+                kept_p[slot, a:b, :] = -share * (p + COARSE * coarse_q)
                 half = KEEP * q - kick[0, a:b, :] * spring + load[a:b, :] * g[0]
                 pos[slot, PAD + a : PAD + b, :] = p + TIME_STEP * half
                 vel[slot, a:b, :] = half
 
             return finish
 
-        def end(n):
+        def end(slot):
             def finish(a, b, new_p, new_q):
-                diff_p[n, PAD + a : PAD + b, :] += new_p
-                diff_q[n, a:b, :] += new_q
+                kept_p[slot, a:b, :] += new_p
+                kept_q[slot, a:b, :] += new_q
 
             return finish
 
@@ -415,22 +426,25 @@
         todo = [(slot, n, gusts(n)) for slot, n in enumerate(slices)]
         stencils([(pos, slot, 0, begin(slot, n, g)) for slot, n, g in todo])
         for i in range(1, FINE):
-            stencils([(pos, slot, 0 if i < 3 else 8, move(slot, g, i)) for slot, n, g in todo])
-        stencils([(pos, slot, 8, close(slot, g, end(n))) for slot, n, g in todo])
+            stencils([(pos, slot, 0 if i < 3 else 8, move(slot, slot, g, i)) for slot, n, g in todo])
+        stencils([(pos, slot, 8, close(slot, g, end(slot))) for slot, n, g in todo])
+        for slot, n, _ in todo:
+            diff_p[n, PAD : PAD + REGION, :] = kept_p[slot]
+            diff_q[n] = kept_q[slot]
 
     own_gust.wait()
     forward(nth(0))
+    first_sweep([nth(0)])
     forward(nth(1))
     forward(nth(2))
-    first_sweep([nth(0)])
 
     def pair(k, carry):
         i = 2 * k + 1
 
-        @pl.when(k < (last - 1) // 2 - 1)
-        def _():
-            forward(nth(i + 2))
-            forward(nth(i + 3))
+        @pl.when(k == 1)
+        def _():
+            for later in range(3, last):
+                forward(nth(later))
 
         first_sweep([nth(i), nth(i + 1)])
         return carry
@@ -462,62 +476,74 @@
         stage(0, a, b, diff_p[0, PAD + a : PAD + b, :], diff_q[0, a:b, :])
     send_back(0)
 
-    lows = {n: [(10 + 2 * n + 2 * k) // 8 * 8 for k in range(FINE + 1)] for n in range(1, tcount)}
-
-    def begin(n):
-        g = gusts(n)
+    def begin(k):
+        g = gusts(k)
 
         def finish(a, b, spring):
-            p = diff_p[n - 1, PAD + a : PAD + b, :]
-            q = diff_q[n - 1, a:b, :]
-            if n < last:
-                coarse_q = KEEP_COARSE * q - kick[2, a:b, :] * spring
-                diff_q[n, a:b, :] += coarse_q
-                diff_p[n, PAD + a : PAD + b, :] += p + COARSE * coarse_q
+            p = chain_p[0, PAD + a : PAD + b, :]
+            q = chain_q[a:b, :]
+            coarse_q = KEEP_COARSE * q - kick[2, a:b, :] * spring
+            next_q = diff_q[k, a:b, :] + coarse_q
+            next_p = diff_p[k, PAD + a : PAD + b, :] + (p + COARSE * coarse_q)
+            chain_q[a:b, :] = next_q
+            chain_p[0, PAD + a : PAD + b, :] = next_p
             half = KEEP * q - kick[0, a:b, :] * spring + load[a:b, :] * g[0]
-            pos[n, PAD + a : PAD + b, :] = p + TIME_STEP * half
-            vel[n, a:b, :] = half
+            pos[0, PAD + a : PAD + b, :] = p + TIME_STEP * half
+            vel[0, a:b, :] = half
 
         return finish
 
-    def correct(slot):
-        def finish(a, b, spring):
-            coarse_q = KEEP_COARSE * corr_q[slot, a:b, :] - kick[2, a:b, :] * spring
-            corr_q[slot, a:b, :] = coarse_q
-            corr_p[slot, PAD + a : PAD + b, :] += COARSE * coarse_q
+    def correct(a, b, spring):
+        coarse_q = KEEP_COARSE * corr_q[a:b, :] - kick[2, a:b, :] * spring
+        corr_q[a:b, :] = coarse_q
+        corr_p[0, PAD + a : PAD + b, :] += COARSE * coarse_q
+
+    def end(n):
+        def finish(a, b, new_p, new_q):
+            new_p = new_p + corr_p[0, PAD + a : PAD + b, :]
+            new_q = new_q + corr_q[a:b, :]
+            corr_p[0, PAD + a : PAD + b, :] = new_p - history[n, 0, a:b, :]
+            corr_q[a:b, :] = new_q - history[n, 1, a:b, :]
+            closed[0, a:b, :] = new_p
+            closed[1, a:b, :] = new_q
 
         return finish
 
-    def end(n):
-        slot = n % 2
-
-        def finish(a, b, new_p, new_q):
-            if n > 1:
-                new_p = new_p + corr_p[slot, PAD + a : PAD + b, :]
-                new_q = new_q + corr_q[slot, a:b, :]
-            if n < last:
-                corr_p[1 - slot, PAD + a : PAD + b, :] = new_p - diff_p[n, PAD + a : PAD + b, :]
-                corr_q[1 - slot, a:b, :] = new_q - diff_q[n, a:b, :]
-            stage(n, a, b, new_p, new_q)
-
-        return finish
-
-    for turn in range(1, tcount + FINE):
+    def turn(k, lo, stages):
         work = []
-        if turn < tcount:
-            work.append((diff_p, turn - 1, lows[turn][0], begin(turn)))
-        for i in range(1, FINE):
-            n = turn - i
-            if 1 <= n < tcount:
-                work.append((pos, n, lows[n][i], move(n, gusts(n), i)))
-        n = turn - FINE
-        if n >= 1:
-            if n > 1:
-                work.append((corr_p, n % 2, lows[n][FINE], correct(n % 2)))
-            work.append((pos, n, lows[n][FINE], close(n, gusts(n), end(n))))
+        if FINE in stages:
+            n = k - FINE
+            work.append((corr_p, 0, lo, correct))
+            work.append((pos, FINE - 1, lo, close(FINE - 1, gusts(n), end(n))))
+        for i in reversed(range(1, FINE)):
+            if i in stages:
+                work.append((pos, i - 1, lo, move(i - 1, i, gusts(lax.rem(k - i + tcount, tcount)), i)))
+        if 0 in stages:
+            work.append((chain_p, 0, lo, begin(k)))
         stencils(work)
-        if n >= 1:
-            send_back(n)
+        if 0 in stages:
+            history[k, 0, lo : REGION - lo, :] = chain_p[0, PAD + lo : PAD + REGION - lo, :]
+            history[k, 1, lo : REGION - lo, :] = chain_q[lo : REGION - lo, :]
+        if FINE in stages:
+            stage(k - FINE, HALO, HALO + STRIP, closed[0, HALO : HALO + STRIP, :], closed[1, HALO : HALO + STRIP, :])
+            send_back(k - FINE)
+
+    def turns(first, end_turn, stages):
+        def step(k, carry):
+            turn(k, (10 + 2 * first) // 8 * 8, stages)
+            return carry
+
+        lax.fori_loop(first, end_turn, step, 0)
+
+    chain_p[...] = diff_p[0:1]
+    chain_q[...] = diff_q[0]
+    corr_p[...] = jnp.zeros_like(corr_p)
+    corr_q[...] = jnp.zeros_like(corr_q)
+    for k in range(1, FINE + 1):
+        turn(k, (10 + 2 * k) // 8 * 8, range(k))
+    turns(FINE + 1, tcount, range(FINE + 1))
+    for k in range(tcount, tcount + FINE):
+        turn(k, (10 + 2 * k) // 8 * 8, range(k - tcount + 1, FINE + 1))
 
     def place(tt, block):
         cols = pl.ds(pl.multiple_of(tt * STRIP, STRIP), STRIP)
@@ -602,12 +628,18 @@
             vmem((REGION, 128), f32),
             vmem((3, REGION, 128), f32),
             vmem((REGION, 128), f32),
+            vmem((FINE, padded, 128), f32),
+            vmem((FINE, REGION, 128), f32),
+            vmem((6, padded, 128), f32),
             vmem((tcount, padded, 128), f32),
             vmem((tcount, REGION, 128), f32),
-            vmem((6, padded, 128), f32),
-            vmem((tcount - 1, padded, 128), f32),
-            vmem((tcount - 1, REGION, 128), f32),
-            vmem((2, padded, 128), f32),
+            vmem((1, padded, 128), f32),
+            vmem((REGION, 128), f32),
+            vmem((1, padded, 128), f32),
+            vmem((REGION, 128), f32),
+            vmem((2, REGION, 128), f32),
+            vmem((tcount, 2, REGION, 128), f32),
+            vmem((2, REGION, 128), f32),
             vmem((2, REGION, 128), f32),
             vmem((tcount, STRIP, 128), f32),
             vmem((tcount, STRIP, 128), f32),

time: 45.6 us -> 44 us (0.965)
  the two profiles are of different devices: /device:TPU:7 before, /device:TPU:390 now
where the time goes in v4:
time: 44 us; the launch traced here: 43.9 us
  Pallas kernels  43.1 us (98%)
  local copies, waits for them, and re-layouts  0.8 us (2%)
    pallas_call x1, Pallas kernels, per_device(): pl.pallas_call(functools.partial(kernel, tcount, scount), out_shape=pltpu...  43.1 us

profile of v4, /device:TPU:390, one launch (start us, length us, event | category | flops | bytes accessed | tf_op | source)
XLA Modules:
  0.0 43.9 jit_solution(1815703250294427482)
XLA Ops:
  0.0 43.1 %shard_map.82 = f32[128,1024]{1,0:T(8,128)S(1)} custom-call(f32[128,1024]{1,0:T(8,128)} %bitcast.4, f32[64,1024]{1,0:T(8,128)} %rigidity.1, f32[64,1024]{1,0:T(8,128)} %inv_mass.1, f32[64,1024]{1,0:T(8,128)} %gust_load.1, f32[4,4]{1,0:T(4,128)} %kl_coeff.1, f32[1,4]{1,0:T(1,128)} %bitcast.5, f32[64,8,128]{2,1,0:T(8,128)} %constant.4.clone.cos_x, ...), custom_call_target="tpu_custom_call" | custom-call | tf_op jit(solution)/shard_map/pallas_call | solution.py:605
  43.1 0.8 %copy.10 = f32[1,2,64,1024]{3,2,1,0:T(8,128)} copy(f32[1,2,64,1024]{3,2,1,0:T(8,128)S(1)} %bitcast.3) | data formatting | bytes 1048576

commit v5 on v4

--- a/solution.py
+++ b/solution.py
@@ -195,28 +195,32 @@
             jnp.where(upper, near, pltpu.roll(further, 96, 1)),
         )
 
+    pl.semaphore_wait(barrier, tcount + tcount * has_far.astype(jnp.int32))
+
+    def send_core(i):
+        tt = lax.rem(t + reversed_bits(i), tcount)
+        gust_copy(tt, t).start()
+
+        @pl.when(t < last)
+        def _():
+            core_copy(tt, t).start()
+
+    def send_far(i):
+        tt = lax.rem(t + reversed_bits(i), tcount)
+
+        @pl.when(jnp.logical_and(t < last, has_far))
+        def _():
+            far_copy(tt, t).start()
+
+    own_copy.start()
+    own_gust.start()
+    for i in range(1, 4):
+        send_core(i)
     for a, b in chunks(0, halo.shape[0]):
         halo[a:b, :] = pack(turned[a:b, :], turned[HALF + a : HALF + b, :])
 
-    pl.semaphore_wait(barrier, tcount + tcount * has_far.astype(jnp.int32))
-
-    def send_to(i):
-        tt = lax.rem(t + reversed_bits(i), tcount)
-        if i > 0:
-            gust_copy(tt, t).start()
-
-            @pl.when(t < last)
-            def _():
-                core_copy(tt, t).start()
-
-        @pl.when(jnp.logical_and(t < last, has_far))
-        def _():
-            far_copy(tt, t).start()
-
-    own_copy.start()
-    own_gust.start()
-    send_to(0)
-    send_to(1)
+    send_far(0)
+    send_far(1)
 
     for copy in loads:
         copy.wait()
@@ -258,7 +262,9 @@
         coef_away.start()
 
     for i in range(2, tcount):
-        send_to(i)
+        if i >= 4:
+            send_core(i)
+        send_far(i)
 
     own_copy.wait()
 

time: 44 us -> 44.4 us (level)
  the two profiles are of different devices: /device:TPU:390 before, /device:TPU:7 now
where the time goes in v5:
time: 44.4 us; the launch traced here: 43.7 us
  Pallas kernels  42.9 us (97%)
  local copies, waits for them, and re-layouts  0.8 us (2%)
    pallas_call x1, Pallas kernels, per_device(): pl.pallas_call(functools.partial(kernel, tcount, scount), out_shape=pltpu...  42.9 us

profile of v5, /device:TPU:7, one launch (start us, length us, event | category | flops | bytes accessed | tf_op | source)
XLA Modules:
  0.0 43.7 jit_solution(9324388377551345572)
XLA Ops:
  0.0 42.9 %shard_map.82 = f32[128,1024]{1,0:T(8,128)S(1)} custom-call(f32[128,1024]{1,0:T(8,128)} %bitcast.4, f32[64,1024]{1,0:T(8,128)} %rigidity.1, f32[64,1024]{1,0:T(8,128)} %inv_mass.1, f32[64,1024]{1,0:T(8,128)} %gust_load.1, f32[4,4]{1,0:T(4,128)} %kl_coeff.1, f32[1,4]{1,0:T(1,128)} %bitcast.5, f32[64,8,128]{2,1,0:T(8,128)} %constant.4.clone.cos_x, ...), custom_call_target="tpu_custom_call" | custom-call | tf_op jit(solution)/shard_map/pallas_call | solution.py:611
  42.9 0.8 %copy.10 = f32[1,2,64,1024]{3,2,1,0:T(8,128)} copy(f32[1,2,64,1024]{3,2,1,0:T(8,128)S(1)} %bitcast.3) | data formatting | bytes 1048576
